TPU v7x, 32 devices: a whole 2x2x4 slice. The times are simulated.
32 devices in a mesh: rows: 16 (over z, y, x), grp: 2 (over core).
Axes of the slice: x: 2, y: 2, z: 4, core: 2. Of those that a mesh axis runs over, the one named last changes fastest.
Arguments:
- latent: float32 [8, 192, 512], P('grp', 'rows'), may hold values from -6 to 6
- w_first: float32 [2, 9, 32, 1], replicated, may hold values from -2 to 2
- b_first: float32 [2, 32], replicated, may hold values from -3 to 3
- w_mid: bfloat16 [2, 9, 32, 32], replicated, may hold values from -0.375 to 0.375
- b_mid: float32 [2, 32], replicated, may hold values from -3 to 3
- w_last: bfloat16 [2, 9, 2, 32], replicated, may hold values from -0.375 to 0.375
- b_last: float32 [2, 2], replicated, may hold values from -3 to 3
- vis_u: int32 [65536], replicated, may hold values from 0 to 191
- vis_v: int32 [65536], replicated, may hold values from 0 to 511
- observed: float32 [2, 65536], replicated, may hold values from -6 to 6
- vis_weight: float32 [65536], replicated, may hold values from 0.25 to 4
Outputs:
- images: float32 [8, 192, 512], P('grp', 'rows')
- loss: float32 [], replicated
- grad_first: float32 [2, 9, 32, 1], replicated
- grad_mid: float32 [2, 9, 32, 32], replicated
- grad_last: float32 [2, 9, 2, 32], replicated
- grad_bias_first: float32 [2, 32], replicated
- grad_bias_mid: float32 [2, 32], replicated
- grad_bias_last: float32 [2, 2], replicated
All inputs are finite; a program needn't handle non-finite values.
Results may differ from a plain program's by a relative error of at most 0.0023.
Values may be sent and summed in bfloat16 or wider, within the bound.
No kernel may reach another device: no remote copies, remote signals or barrier semaphores. Data moves between devices by JAX's collectives and lax.ppermute only.
A program may use at most 320 MiB of HBM per device.

v0:
```python
import functools
import math

import jax
import jax.numpy as jnp
import numpy as np
from jax import lax
from jax.experimental import pallas as pl
from jax.experimental.pallas import tpu as pltpu
from jax.sharding import PartitionSpec as P


BF = jnp.bfloat16
F32 = jnp.float32
GROUP = 4
LANE = 128
SLOT = 40
PLAN = (
    dict(o1=-10, n1=8, o2=-9, n2=8, h1=(2, 5), h2=(2, 4), s1=(2, 4), s2=(2, 4)),
    dict(o1=-7, n1=7, o2=-6, n2=6, h1=(1, 5), h2=(1, 4), s1=(1, 5), s2=(0, 6)),
)


def dot(a, b, dims=((1,), (0,))):
    return lax.dot_general(a, b, (dims, ((), ())), preferred_element_type=F32)


NT = ((1,), (1,))
TN = ((0,), (0,))


def split(x):
    high = x.astype(BF)
    return high, (x - high.astype(F32)).astype(BF)


def dot3(a, b, dims):
    return dot(a[0], b[0], dims) + dot(a[1], b[0], dims) + dot(a[0], b[1], dims)


def down(x):
    rows = lax.broadcasted_iota(jnp.int32, x.shape, 0)
    return jnp.where(rows == 0, 0.0, pltpu.roll(x, 1, 0))


def up(x):
    rows = lax.broadcasted_iota(jnp.int32, x.shape, 0)
    return jnp.where(rows == x.shape[0] - 1, 0.0, pltpu.roll(x, x.shape[0] - 1, 0))


def lane_ids(count):
    return lax.broadcasted_iota(jnp.int32, (1, count), 1)


def taps(cond):
    return down(cond) + pltpu.roll(cond, SLOT, 1) + pltpu.roll(up(cond), 2 * SLOT, 1)


def blk(start, count=1):
    return slice(start * LANE, (start + count) * LANE)


def forward_kernel(height, own, channels, r_ref, lat_ref, wf_a, wf_b, bf_ref, wm_ref, bm_ref, wl_a, wl_b, bl_ref,
                   basis_ref, img_ref, col_ref, logdet_ref, *rest):
    saved, scratch = rest[:-4], rest[-4:]
    hm, h0, hp, h2s = scratch
    first = r_ref[0] * own
    lane = lane_ids(LANE)
    image_row = lane - own + first
    image_mask = ((lane < 3 * own) & (image_row >= 0) & (image_row < height)).astype(F32)
    own_mask = ((lane >= own) & (lane < 2 * own)).astype(F32)

    @pl.when(pl.program_id(0) == 0)
    def _():
        logdet_ref[...] = jnp.zeros_like(logdet_ref)

    def mask_of(origin, block):
        row = origin + block * GROUP + lane // channels + first
        return ((row >= 0) & (row < height)).astype(F32)

    halves = [lat_ref[0, 0], lat_ref[0, 1]]
    for layer, (wf, wl) in enumerate(((wf_a, wl_a), (wf_b, wl_b))):
        plan = PLAN[layer]
        out_h1, out_h2, out_s1, out_s2, out_log = saved[5 * layer : 5 * layer + 5]
        cond, target = halves[layer], halves[1 - layer]
        if layer == 1:
            saved[10][0] = cond
        high, low = split(taps(cond))
        both = jnp.concatenate([high, low], axis=1)
        for k in range(plan["n1"]):
            if k % 2 == 0:
                lanes = blk(k, min(2, plan["n1"] - k))
                pair = dot(both, wf[: 2 * LANE, lanes]) + dot(high, wf[2 * LANE :, lanes])
            pre = pair[:, blk(k % 2)] + bf_ref[layer : layer + 1]
            sig = 0.5 + 0.5 * jnp.tanh(0.5 * pre)
            mask = mask_of(plan["o1"], k)
            hidden = pre * sig * mask
            start, count = plan["s1"]
            if start <= k < start + count:
                out_s1[0, :, blk(k - start)] = sig * (1.0 + pre * (1.0 - sig)) * mask
            plain = hidden.astype(BF)
            h0[:, blk(k)] = plain
            hm[:, blk(k)] = down(hidden).astype(BF)
            hp[:, blk(k)] = up(hidden).astype(BF)
            start, count = plan["h1"]
            if start <= k < start + count:
                out_h1[0, :, blk(k - start)] = plain
        for k in range(plan["n2"]):
            wide = min(2, plan["n1"] - k)
            pre = bm_ref[layer : layer + 1]
            for tap, part in enumerate((hm, h0, hp)):
                pre = pre + dot(part[:, blk(k, wide)], wm_ref[layer, tap, : wide * LANE])
            sig = 0.5 + 0.5 * jnp.tanh(0.5 * pre)
            mask = mask_of(plan["o2"], k)
            hidden = (pre * sig * mask).astype(BF)
            start, count = plan["s2"]
            if start <= k < start + count:
                out_s2[0, :, blk(k - start)] = sig * (1.0 + pre * (1.0 - sig)) * mask
            h2s[:, blk(k)] = hidden
            start, count = plan["h2"]
            if start <= k < start + count:
                out_h2[0, :, blk(k - start)] = hidden
        terms = dot(h2s[:, blk(0, plan["n2"])], wl[...])
        raw = down(terms[:, blk(0)]) + terms[:, blk(1)] + up(terms[:, blk(2)])
        raw = raw + bl_ref[layer : layer + 1]
        log_scale = jnp.tanh(raw)
        out_log[0] = log_scale
        logdet_ref[...] += jnp.sum(log_scale * own_mask, axis=0, keepdims=True)
        halves[1 - layer] = (target * jnp.exp(log_scale) + pltpu.roll(raw, LANE // 2, 1)) * image_mask
    cols = halves[0].shape[0]
    acc = None
    for side in range(2):
        mine = pltpu.roll(halves[side], LANE - own, 1).T
        img_ref[0, :, side * cols : (side + 1) * cols] = mine[:own]
        part = split(mine[:16])
        rows = slice(side * cols, (side + 1) * cols)
        term = dot3(part, (basis_ref[0, rows], basis_ref[1, rows]), ((1,), (0,)))
        acc = term if acc is None else acc + term
    col_ref[0] = acc[:own]


def backward_kernel(height, own, channels, reach, cells, r_ref, near_ref, lat_ref, loss_ref, wf_a, wf_b, wt_ref,
                    wl_a, wl_b, basis_ref, *rest):
    saved, out_ref, scratch = rest[:11], rest[11], rest[12:]
    near_s, dm, d0, dp, cpo_s, acc_mid, acc_last, acc_first, acc_bias = scratch
    step = pl.program_id(0)
    first = r_ref[0] * own
    lane = lane_ids(LANE)
    image_row = lane - own + first
    image_mask = ((lane < 3 * own) & (image_row >= 0) & (image_row < height)).astype(F32)
    raw_row = lane % (LANE // 2)
    own_mask = ((raw_row >= own) & (raw_row < 2 * own)).astype(F32)

    @pl.when(step == 0)
    def _():
        near_s[...] = jnp.zeros_like(near_s)
        for ref in (acc_mid, acc_last, acc_first, acc_bias):
            ref[...] = jnp.zeros_like(ref)

    def own_of(origin, block):
        row = origin + block * GROUP + lane // channels
        return ((row >= 0) & (row < own)).astype(F32)

    near_s[own - reach : 2 * own + reach, :] = near_ref[0]
    near = split(near_s[...])
    cols = lat_ref.shape[2]
    cots = []
    for side in range(2):
        rows = slice(side * cols, (side + 1) * cols)
        cots.append(dot3((basis_ref[0, rows], basis_ref[1, rows]), near, NT))
    cond_one = saved[10][0]
    for layer, wf, wl in ((1, wf_b, wl_b), (0, wf_a, wl_a)):
        plan = PLAN[layer]
        h1, h2, s1, s2, log_ref = saved[5 * layer : 5 * layer + 5]
        cond = cond_one if layer == 1 else lat_ref[0, 0]
        target = lat_ref[0, 1 - layer]
        cot_new = cots[1 - layer]
        log_scale = log_ref[0]
        cot_log = cot_new * target * jnp.exp(log_scale) - 1.0 / cells
        scale_part = cot_log * (1.0 - log_scale * log_scale) * image_mask
        raw = scale_part + pltpu.roll(cot_new * image_mask, LANE // 2, 1)
        raw = raw.astype(BF).astype(F32)
        mine = raw * own_mask
        spread = jnp.concatenate([up(raw).astype(BF), raw.astype(BF), down(raw).astype(BF)], 1)
        spread_own = jnp.concatenate([up(mine).astype(BF), mine.astype(BF), down(mine).astype(BF)], 1)
        acc_last[layer] += dot(spread_own, h2[0], TN)
        acc_bias[layer, 2:3] += jnp.sum(mine, axis=0, keepdims=True)
        start2, count2 = plan["s2"]
        base1, _ = plan["h1"]
        for k in range(start2, start2 + count2):
            cot = dot(spread, wl[blk(k), :], NT) * s2[0, :, blk(k - start2)]
            plain = cot.astype(BF)
            cot = plain.astype(F32)
            parts = (up(cot).astype(BF), plain, down(cot).astype(BF))
            for ref, part in zip((dm, d0, dp), parts):
                ref[:, blk(k - start2)] = part
            local = k - base1
            if 0 <= local < 4:
                mask = own_of(plan["o2"], k)
                acc_bias[layer, 1:2] += jnp.sum(cot * mask, axis=0, keepdims=True)
                lhs = jnp.concatenate([part * mask.astype(BF) for part in parts], 1)
                acc_mid[layer] += dot(lhs, h1[0, :, blk(local, 2)], TN)
        high, low = split(taps(cond))
        start1, count1 = plan["s1"]
        for k in range(start1, start1 + count1):
            back = min(1, k - start2)
            cot = None
            for tap, ref in enumerate((dm, d0, dp)):
                term = dot(ref[:, blk(k - start2 - back, 1 + back)], wt_ref[layer, tap, (1 - back) * LANE :])
                cot = term if cot is None else cot + term
            plain = (cot * s1[0, :, blk(k - start1)]).astype(BF)
            cpo_s[:, blk(k - start1)] = plain
            if k - start1 < 4:
                mask = own_of(plan["o1"], k)
                mine = plain.astype(F32) * mask
                acc_bias[layer, 0:1] += jnp.sum(mine, axis=0, keepdims=True)
                mine = mine.astype(BF)
                acc_first[layer, :, blk(k - start1)] += dot(high, mine, TN) + dot(low, mine, TN)
        if layer == 1:
            full = cpo_s[:, blk(0, count1)]
            lanes = blk(start1, count1)
            terms = dot(full, wf[:LANE, lanes], NT) + dot(full, wf[2 * LANE :, lanes], NT)
            total = up(terms) + pltpu.roll(terms, LANE - SLOT, 1) * (lane < SLOT).astype(F32)
            total = jnp.where(lane < SLOT, total, 0.0)
            total = total + jnp.where(lane < SLOT, pltpu.roll(down(terms), LANE - 2 * SLOT, 1), 0.0)
            cots[1] = cots[1] + total

    @pl.when(step == pl.num_programs(0) - 1)
    def _():
        out_ref[...] = jnp.zeros_like(out_ref)
        layers = len(PLAN)
        tail = layers * 3 * channels
        fold_row = lax.broadcasted_iota(jnp.int32, (4 * LANE, channels), 0)
        fold_col = lax.broadcasted_iota(jnp.int32, (4 * LANE, channels), 1)
        fold = (fold_row % channels == fold_col).astype(F32)
        hi = lax.Precision.HIGHEST

        def folded(x):
            return jnp.dot(x, fold[: x.shape[1]], precision=hi, preferred_element_type=F32)

        def by_row(ref_value, groups, size, shift):
            shape = (groups * size, 4 * LANE)
            inner = lax.broadcasted_iota(jnp.int32, shape, 0) % size
            row = lax.broadcasted_iota(jnp.int32, shape, 1) // channels
            kept = jnp.where(row - inner == shift, ref_value, 0.0)
            return folded(jnp.sum(kept.reshape(groups, size, 4 * LANE), axis=1))

        for layer, plan in enumerate(PLAN):
            for dr in range(3):
                at = (layer * 3 + dr) * channels
                for dc in range(3):
                    total = None
                    for r in range(GROUP):
                        piece = acc_mid[layer, dc * LANE + r * channels : dc * LANE + (r + 1) * channels,
                                        (r + dr) * channels : (r + dr + 1) * channels]
                        total = piece if total is None else total + piece
                    out_ref[at : at + channels, dc * channels : (dc + 1) * channels] = total
                at = tail + (layer * 3 + dr) * 8
                shift = dr - 1 - own - plan["o2"] - GROUP * plan["h2"][0]
                out_ref[at : at + 6, :channels] = by_row(acc_last[layer], 6, LANE // 2, shift)
                shift = 1 - dr - own - plan["o1"] - GROUP * plan["s1"][0]
                out_ref[at : at + 3, channels : 2 * channels] = by_row(
                    acc_first[layer, : 3 * SLOT], 3, SLOT, shift)
            at = tail + layer * 24
            out_ref[at : at + 2, 2 * channels : 3 * channels] = folded(acc_bias[layer, 0:2])
            bias = acc_bias[layer, 2:3]
            pick = lane_ids(channels)
            low = jnp.sum(jnp.where(lane < LANE // 2, bias, 0.0), axis=1, keepdims=True)
            top = jnp.sum(jnp.where(lane >= LANE // 2, bias, 0.0), axis=1, keepdims=True)
            out_ref[at + 2 : at + 3, 2 * channels : 3 * channels] = jnp.where(
                pick == 0, low, jnp.where(pick == 1, top, jnp.where(pick == 2, loss_ref[...], 0.0)))


def prepare_kernel(own, first_ref, mid_ref, last_ref, bf_ref, bm_ref, bl_ref, wf_a, wf_b, wm_ref, wt_ref, wl_a, wl_b,
                   bf_out, bm_out, bl_out):
    channels = mid_ref.shape[2]
    lane = lane_ids(LANE)

    def tiled(x):
        return jnp.concatenate([x] * GROUP, axis=1)

    bf_out[...] = tiled(bf_ref[...])
    bm_out[...] = tiled(bm_ref[...])
    bl_out[...] = jnp.where(lane < LANE // 2, bl_ref[:, 0:1], bl_ref[:, 1:2])
    spread = (lax.broadcasted_iota(jnp.int32, (channels, LANE), 0) == lane % channels).astype(BF)
    parts = lax.broadcasted_iota(jnp.int32, (8, 3 * LANE), 0)
    parts = (parts == lax.broadcasted_iota(jnp.int32, (8, 3 * LANE), 1) // (LANE // 2)).astype(BF)
    wide_lane = lane_ids(3 * LANE) % (LANE // 2)
    edge = lax.broadcasted_iota(jnp.int32, (SLOT, LANE), 0)
    for layer, (wf, wl) in enumerate(((wf_a, wl_a), (wf_b, wl_b))):
        plan = PLAN[layer]
        rows = tiled(first_ref[layer])
        for k in range(plan["n1"]):
            row = k * GROUP + lane // channels + plan["o1"] + own - 1
            pieces = []
            for dc in range(3):
                total = jnp.zeros((SLOT, LANE), F32)
                for dr in range(3):
                    hit = (edge == row + dr) & (edge < 3 * own)
                    total = total + jnp.where(hit, rows[3 * dr + dc : 3 * dr + dc + 1], 0.0)
                pieces.append(total)
            pieces.append(jnp.zeros((LANE - 3 * SLOT, LANE), F32))
            high, low = split(jnp.concatenate(pieces, axis=0))
            wf[:LANE, blk(k)] = high
            wf[LANE : 2 * LANE, blk(k)] = high
            wf[2 * LANE :, blk(k)] = low
        for dc in range(3):
            taps_t = [dot(mid_ref[layer, 3 * dr + dc], spread, TN) for dr in range(3)]
            band = []
            for row in range(2 * GROUP):
                total = jnp.zeros((channels, LANE), F32)
                for dr in range(3):
                    if 0 <= row - dr < GROUP:
                        total = total + jnp.where(lane // channels == row - dr, taps_t[dr], 0.0)
                band.append(total)
            top = jnp.concatenate(band[:GROUP], axis=0)
            low = jnp.concatenate(band[GROUP:], axis=0)
            wm_ref[layer, dc, :LANE] = top.astype(BF)
            wm_ref[layer, dc, LANE:] = low.astype(BF)
            wt_ref[layer, dc, :LANE] = low.T.astype(BF)
            wt_ref[layer, dc, LANE:] = top.T.astype(BF)
        columns = [dot(last_ref[layer, dr], parts, TN) for dr in range(3)]
        for row in range(plan["n2"] * GROUP):
            total = jnp.zeros((channels, 3 * LANE), F32)
            for dr in range(3):
                hit = (wide_lane == row + own + 1 - dr + plan["o2"]) & (wide_lane < 3 * own)
                total = total + jnp.where(hit, columns[dr], 0.0)
            wl[row * channels : (row + 1) * channels, :] = total.astype(BF)


def prepared(w_first, w_mid, w_last, b_first, b_mid, b_last, own):
    layers, channels = b_first.shape
    last = jnp.pad(w_last.reshape(layers, 3, 6, channels), ((0, 0), (0, 0), (0, 2), (0, 0)))
    vmem = pl.BlockSpec(memory_space=pltpu.VMEM)
    shapes = [((3 * LANE, plan["n1"] * LANE), BF) for plan in PLAN]
    shapes += [((layers, 3, 2 * LANE, LANE), BF)] * 2
    shapes += [((plan["n2"] * LANE, 3 * LANE), BF) for plan in PLAN]
    shapes += [((layers, LANE), F32)] * 3
    return pl.pallas_call(
        functools.partial(prepare_kernel, own),
        out_shape=tuple(jax.ShapeDtypeStruct(shape, kind) for shape, kind in shapes),
        in_specs=[vmem] * 6,
        out_specs=tuple(vmem for shape in shapes),
        compiler_params=pltpu.CompilerParams(vmem_limit_bytes=48 * 2**20),
    )(w_first.reshape(layers, 9, channels), w_mid, last, b_first, b_mid, b_last)


def butterfly(value):
    for axis in ("grp", "rows"):
        count = lax.axis_size(axis)
        hop = 1
        while hop < count:
            value = value + lax.ppermute(value, axis, [(i, i ^ hop) for i in range(count)])
            hop *= 2
    return value


def grid_kernel(n_freq, pad_freq, height, img_width, r_ref, u_ref, v_ref, obs_ref, w_ref, sel_ref,
                out_ref, const_ref, u_s, c_s, f_s, acc):
    steps, width = u_ref.shape
    half = img_width // 2
    base = r_ref[0] * n_freq
    u = u_ref[...]
    v = v_ref[...]
    mirror = v > half
    v_fold = jnp.where(mirror, img_width - v, v)
    u_fold = jnp.where(mirror, jnp.where(u == 0, 0, height - u), u)
    col = v_fold - base
    col = jnp.where((col < 0) | (col >= n_freq), pad_freq, col)
    col = jnp.where(v_fold == half, n_freq, col)
    w = w_ref[...]
    o_re = obs_ref[0]
    o_im = obs_ref[1]
    const_ref[...] = jnp.sum(w * (o_re * o_re + o_im * o_im), axis=(0, 1), keepdims=True)
    u_s[...] = u_fold
    c_s[...] = col
    f_s[0] = w
    f_s[1] = w * o_re
    f_s[2] = w * jnp.where(mirror, -o_im, o_im)
    acc[...] = jnp.zeros_like(acc)
    ids = lax.broadcasted_iota(jnp.int32, (16, width), 0).astype(jnp.int16)
    one = jnp.ones((16, width), jnp.bfloat16)
    zero = jnp.zeros((16, width), jnp.bfloat16)

    def step(j, carry):
        row = pl.ds(j, 1)
        u_row = jnp.broadcast_to(u_s[row, :], (16, width)).astype(jnp.int16)
        u_hot = [jnp.where(ids + jnp.int16(16 * g) == u_row, one, zero) for g in range(height // 16)]
        u_hot = jnp.concatenate(u_hot, axis=0)
        c_hot = lax.broadcasted_iota(jnp.int32, (pad_freq, width), 0) == c_s[row, :]
        parts = []
        for field in range(3):
            full = f_s[field, row, :]
            high = full.astype(jnp.bfloat16).astype(jnp.float32)
            parts.append(jnp.where(c_hot, high, 0.0).astype(jnp.bfloat16))
            parts.append(jnp.where(c_hot, full - high, 0.0).astype(jnp.bfloat16))
        values = jnp.concatenate(parts, axis=0)
        acc[...] += lax.dot_general(u_hot, values, (((1,), (1,)), ((), ())),
                                    preferred_element_type=jnp.float32)
        return carry

    lax.fori_loop(0, steps, step, 0)
    grid = acc[...]
    for field in range(3):
        out_ref[field] = jnp.dot(grid, sel_ref[field], precision=lax.Precision.HIGHEST,
                                 preferred_element_type=jnp.float32)


def gridded_lanes(vis_u, vis_v, observed, vis_weight, samples, height, img_width, n_rows):
    n_freq = img_width // 2 // n_rows
    pad_freq = 8 * ((n_freq + 8) // 8)
    lanes = 2 * samples * n_freq
    sel = np.zeros((2, 3, 6 * pad_freq, lanes), np.float32)
    for special in range(2):
        for lane in range(lanes):
            part, freq = lane // (samples * n_freq), lane % n_freq
            lone = special == 1 and freq == 0
            slot = n_freq if lone and part == 1 else freq
            fields = (0, 1, 2) if lone else (0, 1 + part, None)
            for out_id, field in enumerate(fields):
                if field is not None:
                    for split in range(2):
                        sel[special, out_id, (2 * field + split) * pad_freq + slot, lane] = 1.0
    index = lax.axis_index("rows")
    chosen = jnp.where(index == 0, jnp.asarray(sel[1]), jnp.asarray(sel[0]))
    width = min(2048, vis_u.shape[0])
    steps = vis_u.shape[0] // width
    vmem = pl.BlockSpec(memory_space=pltpu.VMEM)
    return pl.pallas_call(
        functools.partial(grid_kernel, n_freq, pad_freq, height, img_width),
        out_shape=(jax.ShapeDtypeStruct((3, height, lanes), jnp.float32),
                   jax.ShapeDtypeStruct((1, 1), jnp.float32)),
        in_specs=[pl.BlockSpec(memory_space=pltpu.SMEM)] + [vmem] * 5,
        out_specs=(vmem, vmem),
        scratch_shapes=[pltpu.VMEM((steps, width), jnp.int32), pltpu.VMEM((steps, width), jnp.int32),
                        pltpu.VMEM((3, steps, width), jnp.float32),
                        pltpu.VMEM((height, 6 * pad_freq), jnp.float32)],
        compiler_params=pltpu.CompilerParams(vmem_limit_bytes=48 * 2**20),
        cost_estimate=pl.CostEstimate(flops=2 * height * 256 * vis_u.shape[0],
                                      bytes_accessed=24 * vis_u.shape[0], transcendentals=0),
    )(index[None].astype(jnp.int32), vis_u.reshape(steps, width), vis_v.reshape(steps, width),
      observed.reshape(2, steps, width), vis_weight.reshape(steps, width), chosen)


def column_basis(img_width, n_rows):
    n_freq = img_width // 2 // n_rows
    cols = np.arange(img_width)
    freq = np.arange(img_width // 2)
    angle = 2.0 * np.pi * ((cols[:, None] * freq[None, :]) % img_width) / img_width
    re, im = np.cos(angle), -np.sin(angle)
    im[:, 0] = 1.0 - 2.0 * (cols % 2)
    both = np.stack([re.reshape(img_width, n_rows, n_freq), im.reshape(img_width, n_rows, n_freq)], 2)
    return both.reshape(img_width, img_width).astype(np.float32)


def spectral_kernel(scale, factor, half, n_freq, r_ref, z_ref, cs_ref, grid_ref, near_ref, data_ref):
    height, lanes = z_ref.shape
    lane = lax.broadcasted_iota(jnp.int32, (1, lanes), 1)
    lone = ((lane % n_freq) == 0) & (r_ref[0] == 0)
    sign = jnp.where(lane < half, 1.0, -1.0)
    hi = lax.Precision.HIGHEST
    z = z_ref[...] * scale
    a = jnp.dot(cs_ref[0], z, precision=hi, preferred_element_type=jnp.float32)
    b = jnp.dot(cs_ref[1], z, precision=hi, preferred_element_type=jnp.float32)
    w, t1, t2 = grid_ref[0], grid_ref[1], grid_ref[2]

    def swap(x):
        return jnp.concatenate([x[:, half:], x[:, :half]], axis=1)

    x = jnp.where(lone, a, a + sign * swap(b))
    p = w * x - t1
    q = jnp.where(lone, w * b + t2, -sign * swap(p))
    b_lone = jnp.where(lone, b, 0.0)
    terms = w * (x * x + b_lone * b_lone) - 2.0 * (x * t1 - b_lone * t2)
    data_ref[...] = jnp.sum(terms, axis=(0, 1), keepdims=True)
    near = jnp.dot(cs_ref[2], p, precision=hi, preferred_element_type=jnp.float32)
    near = near + jnp.dot(cs_ref[3], q, precision=hi, preferred_element_type=jnp.float32)
    near_ref[...] = near * (factor * scale)


def spectral(z, lanes_grid, scale, factor, samples):
    height, lanes = z.shape
    ids = np.arange(height)
    angle = 2.0 * np.pi * ((ids[:, None] * ids[None, :]) % height) / height
    cs = np.stack([np.cos(angle), np.sin(angle), np.cos(angle), np.sin(angle)]).astype(np.float32)
    vmem = pl.BlockSpec(memory_space=pltpu.VMEM)
    return pl.pallas_call(
        functools.partial(spectral_kernel, scale, factor, lanes // 2, lanes // (2 * samples)),
        out_shape=(jax.ShapeDtypeStruct((height, lanes), jnp.float32),
                   jax.ShapeDtypeStruct((1, 1), jnp.float32)),
        in_specs=[pl.BlockSpec(memory_space=pltpu.SMEM)] + [vmem] * 3,
        out_specs=(vmem, vmem),
        compiler_params=pltpu.CompilerParams(vmem_limit_bytes=48 * 2**20),
    )(lax.axis_index("rows")[None].astype(jnp.int32), z, jnp.asarray(cs), lanes_grid)


def body(
    latent, w_first, b_first, w_mid, b_mid, w_last, b_last, vis_u, vis_v, observed, vis_weight
):
    samples, row_count, img_width = latent.shape
    half_cols = img_width // 2
    n_rows = lax.axis_size("rows")
    n_grp = lax.axis_size("grp")
    height = row_count * n_rows
    batch_size = samples * n_grp
    layers = w_first.shape[0]
    vis_total = vis_u.shape[0]
    cells = height * img_width
    lanes_grid, obs_const = gridded_lanes(
        vis_u, vis_v, observed, vis_weight, samples, height, img_width, n_rows
    )
    channels = w_mid.shape[2]
    half = half_cols
    forward = [(i, i + 1) for i in range(n_rows - 1)]
    backward = [(target, source) for source, target in forward]
    low = lax.ppermute(latent, "rows", forward)
    high = lax.ppermute(latent, "rows", backward)
    wide = jnp.concatenate([low, latent, high], axis=1)
    wide = wide.reshape(samples, 3 * row_count, 2, half).transpose(0, 2, 3, 1)
    wide = jnp.pad(wide, ((0, 0), (0, 0), (0, 0), (0, LANE - 3 * row_count)))
    wf_a, wf_b, wm, wt, wl_a, wl_b, bias_first, bias_mid, bias_last = prepared(
        w_first, w_mid, w_last, b_first, b_mid, b_last, row_count
    )
    basis_np = column_basis(img_width, n_rows)
    basis_high = basis_np.astype(BF)
    basis_low = (basis_np - basis_high.astype(np.float32)).astype(BF)
    basis = jnp.asarray(np.stack([basis_high, basis_low]))
    index = lax.axis_index("rows")[None].astype(jnp.int32)
    smem = pl.BlockSpec(memory_space=pltpu.SMEM)

    def whole(value):
        rank = value.ndim
        return pl.BlockSpec(value.shape, lambda s: (0,) * rank)

    def per_sample(*shape):
        rank = len(shape)
        return pl.BlockSpec((1,) + shape, lambda s: (s,) + (0,) * rank)

    saved_shapes = []
    for plan in PLAN:
        for key, kind in (("h1", BF), ("h2", BF), ("s1", F32), ("s2", F32)):
            saved_shapes.append(((half, plan[key][1] * LANE), kind))
        saved_shapes.append(((half, LANE), F32))
    saved_shapes.append(((half, LANE), F32))
    saved_specs = [per_sample(*shape) for shape, kind in saved_shapes]
    saved_types = [jax.ShapeDtypeStruct((samples,) + shape, kind) for shape, kind in saved_shapes]
    weights = (wf_a, wf_b, bias_first, wm, bias_mid, wl_a, wl_b, bias_last, basis)
    max1 = max(plan["n1"] for plan in PLAN) * LANE
    max2 = max(plan["n2"] for plan in PLAN) * LANE
    params = pltpu.CompilerParams(vmem_limit_bytes=56 * 2**20)
    image_out, columns, logdet, *saved = pl.pallas_call(
        functools.partial(forward_kernel, height, row_count, channels),
        grid=(samples,),
        out_shape=(
            jax.ShapeDtypeStruct((samples, row_count, img_width), F32),
            jax.ShapeDtypeStruct((samples, row_count, img_width), F32),
            jax.ShapeDtypeStruct((1, LANE), F32),
            *saved_types,
        ),
        in_specs=[smem, per_sample(2, half, LANE)] + [whole(value) for value in weights],
        out_specs=(
            per_sample(row_count, img_width),
            per_sample(row_count, img_width),
            pl.BlockSpec((1, LANE), lambda s: (0, 0)),
            *saved_specs,
        ),
        scratch_shapes=[pltpu.VMEM((half, max1), BF)] * 3 + [pltpu.VMEM((half, max2), BF)],
        compiler_params=params,
    )(index, wide, *weights)
    logdet = jnp.sum(logdet)
    norm_scale = 1.0 / math.sqrt(height * img_width)
    factor = 2.0 / (vis_total * batch_size)
    n_freq = img_width // 2 // n_rows
    columns = columns.reshape(samples, row_count, n_rows, 2, n_freq).transpose(2, 1, 3, 0, 4)
    columns = columns.reshape(n_rows, row_count, 2 * samples * n_freq)
    columns = lax.all_to_all(columns, "rows", 0, 0, tiled=True)
    near, data_sum = spectral(
        columns.reshape(height, 2 * samples * n_freq), lanes_grid, norm_scale, factor, samples
    )
    reach = 6
    blocks = jnp.pad(near.reshape(n_rows, row_count, -1), ((1, 1), (0, 0), (0, 0)))
    blocks = jnp.concatenate(
        [blocks[:-2, row_count - reach :], blocks[1:-1], blocks[2:, :reach]], axis=1
    )
    near = lax.all_to_all(blocks, "rows", 0, 0, tiled=True)
    span = row_count + 2 * reach
    near = near.reshape(n_rows, span, 2, samples, n_freq).transpose(3, 1, 0, 2, 4)
    near = near.reshape(samples, span, img_width)
    data_part = (data_sum[0, 0] + samples * obs_const[0, 0] / n_rows) / vis_total
    loss_part = (data_part - logdet / (height * img_width)) / batch_size
    out_rows = layers * (3 * channels + 24)
    weights = (wf_a, wf_b, wt, wl_a, wl_b, basis)
    flat = pl.pallas_call(
        functools.partial(
            backward_kernel, height, row_count, channels, reach, batch_size * cells
        ),
        grid=(samples,),
        out_shape=jax.ShapeDtypeStruct((out_rows, LANE), F32),
        in_specs=[smem, per_sample(span, img_width), per_sample(2, half, LANE),
                  pl.BlockSpec((1, 1), lambda s: (0, 0))]
        + [whole(value) for value in weights] + saved_specs,
        out_specs=pl.BlockSpec((out_rows, LANE), lambda s: (0, 0)),
        scratch_shapes=[
            pltpu.VMEM((LANE, img_width), F32),
            *[pltpu.VMEM((half, max2), BF)] * 3,
            pltpu.VMEM((half, max1), BF),
            pltpu.VMEM((layers, 3 * LANE, 2 * LANE), F32),
            pltpu.VMEM((layers, 3 * LANE, 4 * LANE), F32),
            pltpu.VMEM((layers, LANE, 4 * LANE), F32),
            pltpu.VMEM((layers, 8, LANE), F32),
        ],
        compiler_params=params,
    )(index, near, wide, loss_part.reshape(1, 1), *weights, *saved)
    flat = butterfly(flat)
    main = flat[: layers * 3 * channels, : 3 * channels]
    main = main.reshape(layers, 3, channels, 3, channels).transpose(0, 1, 3, 2, 4)
    rest = flat[layers * 3 * channels :].reshape(layers, 3, 8, LANE)
    final_grads = [
        rest[:, :, :3, channels : 2 * channels].reshape(layers, 9, channels, 1),
        main.reshape(layers, 9, channels, channels),
        rest[:, :, :6, :channels].reshape(layers, 9, 2, channels),
        rest[:, 0, 0, 2 * channels : 3 * channels],
        rest[:, 0, 1, 2 * channels : 3 * channels],
        rest[:, 0, 2, 2 * channels : 2 * channels + 2],
    ]
    loss = rest[0, 0, 2, 2 * channels + 2]
    return (
        image_out,
        loss,
        final_grads[0],
        final_grads[1],
        final_grads[2],
        final_grads[3],
        final_grads[4],
        final_grads[5],
    )


def solution(mesh):
    in_specs = (P("grp", "rows", None), P(), P(), P(), P(), P(), P(), P(), P(), P(), P())
    out_specs = (P("grp", "rows", None), P(), P(), P(), P(), P(), P(), P())
    return jax.shard_map(body, mesh=mesh, in_specs=in_specs, out_specs=out_specs, check_vma=False)
```

profile of v0, /device:TPU:0, one launch (start us, length us, event | category | flops | bytes accessed | tf_op | source)
XLA Modules:
  0.0 149.9 jit_solution(16547432602114160462)
XLA Ops:
  0.7 5.0 %collective-permute-start = (f32[4,12,512]{2,0,1:T(4,128)}, f32[4,12,512]{2,0,1:T(4,128)S(1)}, u32[]{:S(2)}, u32[]{:S(2)}) collective-permute-start(f32[4,12,512]{2,0,1:T(4,128)} %param.15), channel_id=1, source_target_pairs={{0,2},{2,4},{4,6},{6,8},{8,10},{10,12},{12,14},{14,16},{16,18},{18... | collective-permute-start | bytes 294920 | tf_op jit(solution)/shard_map/ppermute | solution.py:516
  5.7 1.3 collective-permute-start.1
  7.0 1.0 broadcast_select_fusion.sel_ref
  9.4 1.0 reshape.84.u_ref
  10.4 1.0 reshape.85.v_ref
  11.4 1.0 reshape.87.w_ref
  12.8 1.7 %shard_map.206 = (bf16[384,1024]{1,0:T(8,128)(2,1)S(1)}, bf16[384,896]{1,0:T(8,128)(2,1)S(1)}, bf16[2,3,256,128]{3,2,1,0:T(8,128)(2,1)S(1)}, bf16[2,3,256,128]{3...) custom-call(f32[2,9,32]{2,1,0:T(8,128)S(1)} %copy.69.first_ref, ...), custom_call_target="tpu_custom_call" | custom-call | tf_op jit(solution)/shard_map/pallas_call | solution.py:339
  14.5 0.9 copy-done
  15.4 0.9 copy-done.1
  16.3 0.9 copy-done.2
  21.1 1.1 pad.12.lat_ref
  22.2 23.1 %shard_map.207 = (f32[4,12,512]{2,1,0:T(8,128)}, f32[4,12,512]{2,1,0:T(8,128)}, f32[1,128]{1,0:T(1,128)}, bf16[4,256,640]{2,1,0:T(8,128)(2,1)}, bf16[4,256,512]{...) custom-call(s32[1]{0:T(128)} %bitcast.r_ref, ...), custom_call_target="tpu_custom_call" | custom-call | tf_op jit(solution)/shard_map/pallas_call | solution.py:551
  45.3 1.0 copy.70
  46.3 1.1 reshape.81
  47.8 1.2 reshape.97
  49.0 8.0 %all-to-all-start = ((f32[16,12,128]{2,1,0:T(8,128)}), f32[16,12,128]{2,1,0:T(8,128)S(1)}, u32[]{:S(2)}, u32[]{:S(2)}) async-start(f32[16,12,128]{2,1,0:T(8,128)} %reshape.97), calls=%async_computation | async-start | bytes 262144 | tf_op jit(solution)/shard_map/all_to_all | solution.py:576
  57.0 14.3 %shard_map.208 = (f32[3,192,128]{2,1,0:T(8,128)S(1)}, f32[1,1]{1,0:T(1,128)}) custom-call(s32[1]{0:T(128)} %bitcast.r_ref, s32[32,2048]{1,0:T(8,128)S(1)} %reshape.84.u_ref, s32[32,2048]{1,0:T(8,128)S(1)} %reshape.85.v_ref, f32[2,32,2048]{2,1,0:T(8,128)S(1)} %bitcast.34, f32[32,2048]{1,0:T(8,128)S(1)} %reshape.87.w_ref, ...), custom_call_target="tpu_custom_call" | custom-call | flops 6442450944 | bytes 1572864 | tf_op jit(solution)/shard_map/pallas_call | solution.py:429
  71.4 1.8 %shard_map.209 = (f32[192,128]{1,0:T(8,128)S(1)}, f32[1,1]{1,0:T(1,128)}) custom-call(s32[1]{0:T(128)} %bitcast.r_ref, f32[192,128]{1,0:T(8,128)S(1)} %reshape.83.z_ref, f32[4,192,192]{2,1,0:T(8,128)S(1)} %copy-done.4, f32[3,192,128]{2,1,0:T(8,128)S(1)} %get-tuple-element.45.grid_ref), custom_call_target="tpu_custom_call" | custom-call | tf_op jit(solution)/shard_map/pallas_call | solution.py:487
  73.9 6.9 %all-to-all-start.1 = ((f32[16,24,128]{2,1,0:T(8,128)}), f32[16,24,128]{2,1,0:T(8,128)S(1)}, u32[]{:S(2)}, u32[]{:S(2)}) async-start(f32[16,24,128]{2,1,0:T(8,128)} %pad_maximum_fusion.1), calls=%async_computation.1 | async-start | bytes 393216 | tf_op jit(solution)/shard_map/all_to_all | solution.py:585
  83.4 5.5 %all-to-all-done.1 = f32[16,24,128]{2,1,0:T(8,128)S(1)} async-done(((f32[16,24,128]{2,1,0:T(8,128)}), f32[16,24,128]{2,1,0:T(8,128)S(1)}, u32[]{:S(2)}, u32[]{:S(2)}) %all-to-all-start.1) | async-done | bytes 196640 | tf_op jit(solution)/shard_map/all_to_all | solution.py:585
  88.9 1.1 reshape.89
  90.8 3.0 %reshape.90.near_ref = f32[4,24,512]{2,1,0:T(8,128)} reshape(f32[4,24,16,2,16]{4,3,2,1,0:T(2,128)S(1)} %copy.73) | data formatting | bytes 393216 | tf_op jit(solution)/shard_map/reshape | solution.py:588
  93.8 26.9 %shard_map.210 = f32[240,128]{1,0:T(8,128)} custom-call(s32[1]{0:T(128)} %bitcast.r_ref, f32[4,24,512]{2,1,0:T(8,128)} %reshape.90.near_ref, f32[4,2,256,128]{3,2,1,0:T(8,128)} %pad.12.lat_ref, f32[1,1]{1,0:T(1,128)} %bitcast.8.loss_ref, bf16[384,1024]{1,0:T(8,128)(2,1)} %copy-done, bf16[384,896]{1,0:T(8,128)(2,1)} %copy-done.2, ...), custom_call_target="tpu_custom_call" | custom-call | tf_op jit(solution)/shard_map/pallas_call | solution.py:593
  120.7 1.5 %collective-permute-done.2 = f32[240,128]{1,0:T(8,128)S(1)} collective-permute-done((f32[240,128]{1,0:T(8,128)}, f32[240,128]{1,0:T(8,128)S(1)}, u32[]{:S(2)}, u32[]{:S(2)}) %collective-permute-start.2) | collective-permute-done | bytes 122912 | tf_op jit(solution)/shard_map/ppermute | solution.py:353
  122.3 0.9 add.26
  123.2 1.4 collective-permute-start.3
  124.6 4.0 %collective-permute-done.3 = f32[240,128]{1,0:T(8,128)S(1)} collective-permute-done((f32[240,128]{1,0:T(8,128)S(1)}, f32[240,128]{1,0:T(8,128)S(1)}, u32[]{:S(2)}, u32[]{:S(2)}) %collective-permute-start.3) | collective-permute-done | bytes 122912 | tf_op jit(solution)/shard_map/ppermute | solution.py:353
  128.7 0.9 collective-permute-start.4
  129.5 4.1 %collective-permute-done.4 = f32[240,128]{1,0:T(8,128)S(1)} collective-permute-done((f32[240,128]{1,0:T(8,128)S(1)}, f32[240,128]{1,0:T(8,128)S(1)}, u32[]{:S(2)}, u32[]{:S(2)}) %collective-permute-start.4) | collective-permute-done | bytes 122912 | tf_op jit(solution)/shard_map/ppermute | solution.py:353
  134.5 4.1 %collective-permute-done.5 = f32[240,128]{1,0:T(8,128)S(1)} collective-permute-done((f32[240,128]{1,0:T(8,128)S(1)}, f32[240,128]{1,0:T(8,128)S(1)}, u32[]{:S(2)}, u32[]{:S(2)}) %collective-permute-start.5) | collective-permute-done | bytes 122912 | tf_op jit(solution)/shard_map/ppermute | solution.py:353
  138.6 1.1 collective-permute-start.6
  140.4 5.3 %collective-permute-done.6 = f32[240,128]{1,0:T(8,128)S(1)} collective-permute-done((f32[240,128]{1,0:T(8,128)S(1)}, f32[240,128]{1,0:T(8,128)S(1)}, u32[]{:S(2)}, u32[]{:S(2)}) %collective-permute-start.6) | collective-permute-done | bytes 122912 | tf_op jit(solution)/shard_map/ppermute | solution.py:353
  (70 shorter events, 14.2 us)
Async XLA Ops:
  0.6 20.0 %copy-start.16 = (f32[4,12,512]{2,0,1:T(4,128)S(1)}, f32[4,12,512]{2,0,1:T(4,128)}, u32[]{:S(2)}) copy-start(f32[4,12,512]{2,0,1:T(4,128)} %param.15) | copy-start | bytes 294916
  0.6 11.8 %copy-start.14 = (f32[2,65536]{1,0:T(2,128)S(1)}, f32[2,65536]{1,0:T(2,128)}, u32[]{:S(2)}) copy-start(f32[2,65536]{1,0:T(2,128)} %param.24) | copy-start | bytes 1572868
  0.7 12.1 %copy-start.10 = (f32[2,2]{1,0:T(2,128)S(1)}, f32[2,2]{1,0:T(2,128)}, u32[]{:S(2)}) copy-start(f32[2,2]{1,0:T(2,128)} %bl_ref.1) | copy-start | bytes 52
  0.7 12.1 %copy-start.9 = (f32[2,32]{1,0:T(2,128)S(1)}, f32[2,32]{1,0:T(2,128)}, u32[]{:S(2)}) copy-start(f32[2,32]{1,0:T(2,128)} %bm_ref.1) | copy-start | bytes 772
  0.7 12.1 %copy-start.7 = (bf16[2,9,32,32]{3,2,1,0:T(8,128)(2,1)S(1)}, bf16[2,9,32,32]{3,2,1,0:T(8,128)(2,1)}, u32[]{:S(2)}) copy-start(bf16[2,9,32,32]{3,2,1,0:T(8,128)(2,1)} %mid_ref.1) | copy-start | bytes 110596
  0.7 12.1 %copy-start.8 = (f32[2,32]{1,0:T(2,128)S(1)}, f32[2,32]{1,0:T(2,128)}, u32[]{:S(2)}) copy-start(f32[2,32]{1,0:T(2,128)} %bf_ref.1) | copy-start | bytes 772
  0.7 19.9 %collective-permute-start = (f32[4,12,512]{2,0,1:T(4,128)}, f32[4,12,512]{2,0,1:T(4,128)S(1)}, u32[]{:S(2)}, u32[]{:S(2)}) collective-permute-start(f32[4,12,512]{2,0,1:T(4,128)} %param.15), channel_id=1, source_target_pairs={{0,2},{2,4},{4,6},{6,8},{8,10},{10,12},{12,14},{14,16},{16,18},{18... | collective-permute-start | bytes 294920 | tf_op jit(solution)/shard_map/ppermute | solution.py:516
  5.7 14.9 %collective-permute-start.1 = (f32[4,12,512]{2,0,1:T(4,128)}, f32[4,12,512]{2,0,1:T(4,128)S(1)}, u32[]{:S(2)}, u32[]{:S(2)}) collective-permute-start(f32[4,12,512]{2,0,1:T(4,128)} %param.15), channel_id=1, source_target_pairs={{2,0},{4,2},{6,4},{8,6},{10,8},{12,10},{14,12},{16,14},{18,16},{20... | collective-permute-start | bytes 294920 | tf_op jit(solution)/shard_map/ppermute | solution.py:517
  14.5 0.9 copy-start
  15.4 0.9 copy-start.1
  16.3 0.9 copy-start.2
  17.2 0.8 copy-start.3
  18.0 0.8 copy-start.5
  18.7 0.7 copy-start.6
  19.5 0.6 copy-start.11
  20.1 0.6 copy-start.12
  20.6 1.6 %copy-start.13 = (f32[2,128]{1,0:T(2,128)}, f32[2,128]{1,0:T(2,128)S(1)}, u32[]{:S(2)}) copy-start(f32[2,128]{1,0:T(2,128)S(1)} %get-tuple-element.42.bl_ref) | copy-start | bytes 3076
  49.0 22.3 %all-to-all-start = ((f32[16,12,128]{2,1,0:T(8,128)}), f32[16,12,128]{2,1,0:T(8,128)S(1)}, u32[]{:S(2)}, u32[]{:S(2)}) async-start(f32[16,12,128]{2,1,0:T(8,128)} %reshape.97), calls=%async_computation | async-start | bytes 262144 | tf_op jit(solution)/shard_map/all_to_all | solution.py:576
  57.0 14.3 %copy-start.4 = (f32[4,192,192]{2,1,0:T(8,128)S(1)}, f32[4,192,192]{2,1,0:T(8,128)}, u32[]{:S(2)}) copy-start(f32[4,192,192]{2,1,0:T(8,128)} %constant.40.clone.cs_ref) | copy-start | bytes 1769476
  71.3 10.1 %copy-start.17 = (f32[1,128]{1,0:T(1,128)S(1)}, f32[1,128]{1,0:T(1,128)}, u32[]{:S(2)}) copy-start(f32[1,128]{1,0:T(1,128)} %get-tuple-element.49) | copy-start | bytes 1540
  73.9 15.0 %all-to-all-start.1 = ((f32[16,24,128]{2,1,0:T(8,128)}), f32[16,24,128]{2,1,0:T(8,128)S(1)}, u32[]{:S(2)}, u32[]{:S(2)}) async-start(f32[16,24,128]{2,1,0:T(8,128)} %pad_maximum_fusion.1), calls=%async_computation.1 | async-start | bytes 393216 | tf_op jit(solution)/shard_map/all_to_all | solution.py:585
  93.8 45.9 %copy-start.15 = (f32[4,12,512]{2,1,0:T(8,128)S(1)}, f32[4,12,512]{2,1,0:T(8,128)}, u32[]{:S(2)}) copy-start(f32[4,12,512]{2,1,0:T(8,128)} %get-tuple-element.86) | copy-start | bytes 294916
  120.7 1.6 %collective-permute-start.2 = (f32[240,128]{1,0:T(8,128)}, f32[240,128]{1,0:T(8,128)S(1)}, u32[]{:S(2)}, u32[]{:S(2)}) collective-permute-start(f32[240,128]{1,0:T(8,128)} %shard_map.210), channel_id=1, source_target_pairs={{0,1},{1,0},{2,3},{3,2},{4,5},{5,4},{6,7},{7,6},{8,9},{9,8},{10,11... | collective-permute-start | bytes 368648 | tf_op jit(solution)/shard_map/ppermute | solution.py:353
  123.2 5.4 %collective-permute-start.3 = (f32[240,128]{1,0:T(8,128)S(1)}, f32[240,128]{1,0:T(8,128)S(1)}, u32[]{:S(2)}, u32[]{:S(2)}) collective-permute-start(f32[240,128]{1,0:T(8,128)S(1)} %add.26), channel_id=1, source_target_pairs={{0,2},{2,0},{4,6},{6,4},{8,10},{10,8},{12,14},{14,12},{16,18},{18,... | collective-permute-start | bytes 368648 | tf_op jit(solution)/shard_map/ppermute | solution.py:353
  128.7 4.9 %collective-permute-start.4 = (f32[240,128]{1,0:T(8,128)S(1)}, f32[240,128]{1,0:T(8,128)S(1)}, u32[]{:S(2)}, u32[]{:S(2)}) collective-permute-start(f32[240,128]{1,0:T(8,128)S(1)} %add.27), channel_id=1, source_target_pairs={{0,4},{2,6},{4,0},{6,2},{8,12},{10,14},{12,8},{14,10},{16,20},{18,... | collective-permute-start | bytes 368648 | tf_op jit(solution)/shard_map/ppermute | solution.py:353
  133.6 4.9 %collective-permute-start.5 = (f32[240,128]{1,0:T(8,128)S(1)}, f32[240,128]{1,0:T(8,128)S(1)}, u32[]{:S(2)}, u32[]{:S(2)}) collective-permute-start(f32[240,128]{1,0:T(8,128)S(1)} %add.28), channel_id=1, source_target_pairs={{0,8},{2,10},{4,12},{6,14},{8,0},{10,2},{12,4},{14,6},{16,24},{18,... | collective-permute-start | bytes 368648 | tf_op jit(solution)/shard_map/ppermute | solution.py:353
  138.6 7.2 %collective-permute-start.6 = (f32[240,128]{1,0:T(8,128)S(1)}, f32[240,128]{1,0:T(8,128)S(1)}, u32[]{:S(2)}, u32[]{:S(2)}) collective-permute-start(f32[240,128]{1,0:T(8,128)S(1)} %add.29), channel_id=1, source_target_pairs={{0,16},{2,18},{4,20},{6,22},{8,24},{10,26},{12,28},{14,30},{16,0},... | collective-permute-start | bytes 368648 | tf_op jit(solution)/shard_map/ppermute | solution.py:353
where the time goes:
time: 151 us; the launch traced here: 150 us
  Pallas kernels  67.7 us (45%)
  local copies, waits for them, and re-layouts  25.8 us (17%)
  starting transfers between devices  25.5 us (17%)
  waiting for transfers between devices  24.6 us (16%)
  other arithmetic  3.33 us (2%)
  between operations  2.95 us (2%)
    pallas_call x1, Pallas kernels, body(): pl.pallas_call(functools.partial(backward_kernel, height, row_count, chan...  26.9 us
    pallas_call x1, Pallas kernels, body(): pl.pallas_call(functools.partial(forward_kernel, height, row_count, chann...  23.1 us
    ppermute x5, waiting for transfers between devices, butterfly(): lax.ppermute(value, axis, [(i, i ^ hop) for i in range(count)])  19.1 us
    pallas_call x1, Pallas kernels, gridded_lanes(): pl.pallas_call(functools.partial(grid_kernel, n_freq, pad_freq, height, i...  14.3 us
    unnamed x44, local copies, waits for them, and re-layouts  9.84 us
    all_to_all x1, starting transfers between devices, body(): columns = lax.all_to_all(columns, 'rows', 0, 0, tiled=True)  8.02 us
    all_to_all x1, starting transfers between devices, body(): near = lax.all_to_all(blocks, 'rows', 0, 0, tiled=True)  6.91 us
    all_to_all x1, waiting for transfers between devices, body(): near = lax.all_to_all(blocks, 'rows', 0, 0, tiled=True)  5.51 us
  transfers between devices with their start and end apart: 9, of which 6 were waited for; matrix products, arithmetic and copies ran while one was open for 5% of the time, Pallas kernels for 11%

commit v1 on v0

v1 whole, which is shorter than its diff:
```python
import functools
import math

import jax
import jax.numpy as jnp
import numpy as np
from jax import lax
from jax.experimental import pallas as pl
from jax.experimental.pallas import tpu as pltpu
from jax.sharding import PartitionSpec as P


BF = jnp.bfloat16
F32 = jnp.float32
GROUP = 4
LANE = 128
SLOT = 40
PLAN = (
    dict(o1=-10, n1=8, o2=-9, n2=8, h1=(2, 5), h2=(2, 4), s1=(2, 4), s2=(2, 4)),
    dict(o1=-7, n1=7, o2=-6, n2=6, h1=(1, 5), h2=(1, 4), s1=(1, 5), s2=(0, 6)),
)


def dot(a, b, dims=((1,), (0,))):
    return lax.dot_general(a, b, (dims, ((), ())), preferred_element_type=F32)


NT = ((1,), (1,))
TN = ((0,), (0,))


def split(x):
    high = x.astype(BF)
    return high, (x - high.astype(F32)).astype(BF)


def dot3(a, b, dims):
    return dot(a[0], b[0], dims) + dot(a[1], b[0], dims) + dot(a[0], b[1], dims)


def down(x):
    rows = lax.broadcasted_iota(jnp.int32, x.shape, 0)
    return jnp.where(rows == 0, 0.0, pltpu.roll(x, 1, 0))


def up(x):
    rows = lax.broadcasted_iota(jnp.int32, x.shape, 0)
    return jnp.where(rows == x.shape[0] - 1, 0.0, pltpu.roll(x, x.shape[0] - 1, 0))


def lane_ids(count):
    return lax.broadcasted_iota(jnp.int32, (1, count), 1)


def taps(cond):
    return down(cond) + pltpu.roll(cond, SLOT, 1) + pltpu.roll(up(cond), 2 * SLOT, 1)


def blk(start, count=1):
    return slice(start * LANE, (start + count) * LANE)


def forward_kernel(height, own, channels, r_ref, low_ref, mid_ref, high_ref, first_ref, taps_ref, last_ref, b1_ref,
                   b2_ref, b3_ref, basis_ref, img_ref, col_ref, logdet_ref, wf_a, wf_b, wt_ref, wl_a, wl_b, *rest):
    saved, scratch = rest[:-11], rest[-11:]
    wm_ref, bf_ref, bm_ref, bl_ref, hm, h0, hp, h2s, wide_s, lat_s, mine_s = scratch
    step = pl.program_id(0)
    samples, cols = lat_s.shape[0], lat_s.shape[2]
    first = r_ref[0] * own
    lane = lane_ids(LANE)
    image_row = lane - own + first
    image_mask = ((lane < 3 * own) & (image_row >= 0) & (image_row < height)).astype(F32)
    own_mask = ((lane >= own) & (lane < 2 * own)).astype(F32)

    @pl.when(step == 0)
    def _():
        logdet_ref[...] = jnp.zeros_like(logdet_ref)
        prepare(own, first_ref, taps_ref, last_ref, b1_ref, b2_ref, b3_ref, wf_a, wf_b, wm_ref, wt_ref, wl_a, wl_b,
                bf_ref, bm_ref, bl_ref)
        wide_s[...] = jnp.zeros_like(wide_s)
        for s in range(samples):
            for place, ref in enumerate((low_ref, mid_ref, high_ref)):
                wide_s[place * own : (place + 1) * own, :] = ref[:, s, :]
            turned = wide_s[...].T
            for side in range(2):
                lat_s[s, side] = turned[side * cols : (side + 1) * cols]

    def mask_of(origin, block):
        row = origin + block * GROUP + lane // channels + first
        return ((row >= 0) & (row < height)).astype(F32)

    halves = [lat_s[step, 0], lat_s[step, 1]]
    for side in range(2):
        saved[11][0, side] = halves[side]
    for layer, (wf, wl) in enumerate(((wf_a, wl_a), (wf_b, wl_b))):
        plan = PLAN[layer]
        out_h1, out_h2, out_s1, out_s2, out_log = saved[5 * layer : 5 * layer + 5]
        cond, target = halves[layer], halves[1 - layer]
        if layer == 1:
            saved[10][0] = cond
        high, low = split(taps(cond))
        both = jnp.concatenate([high, low], axis=1)
        for k in range(plan["n1"]):
            if k % 2 == 0:
                lanes = blk(k, min(2, plan["n1"] - k))
                pair = dot(both, wf[: 2 * LANE, lanes]) + dot(high, wf[2 * LANE :, lanes])
            pre = pair[:, blk(k % 2)] + bf_ref[layer : layer + 1]
            sig = 0.5 + 0.5 * jnp.tanh(0.5 * pre)
            mask = mask_of(plan["o1"], k)
            hidden = pre * sig * mask
            start, count = plan["s1"]
            if start <= k < start + count:
                out_s1[0, :, blk(k - start)] = (sig * (1.0 + pre * (1.0 - sig)) * mask).astype(BF)
            plain = hidden.astype(BF)
            h0[:, blk(k)] = plain
            hm[:, blk(k)] = down(hidden).astype(BF)
            hp[:, blk(k)] = up(hidden).astype(BF)
            start, count = plan["h1"]
            if start <= k < start + count:
                out_h1[0, :, blk(k - start)] = plain
        for k in range(plan["n2"]):
            wide = min(2, plan["n1"] - k)
            pre = bm_ref[layer : layer + 1]
            for tap, part in enumerate((hm, h0, hp)):
                pre = pre + dot(part[:, blk(k, wide)], wm_ref[layer, tap, : wide * LANE])
            sig = 0.5 + 0.5 * jnp.tanh(0.5 * pre)
            mask = mask_of(plan["o2"], k)
            hidden = (pre * sig * mask).astype(BF)
            start, count = plan["s2"]
            if start <= k < start + count:
                out_s2[0, :, blk(k - start)] = (sig * (1.0 + pre * (1.0 - sig)) * mask).astype(BF)
            h2s[:, blk(k)] = hidden
            start, count = plan["h2"]
            if start <= k < start + count:
                out_h2[0, :, blk(k - start)] = hidden
        terms = dot(h2s[:, blk(0, plan["n2"])], wl[...])
        raw = down(terms[:, blk(0)]) + terms[:, blk(1)] + up(terms[:, blk(2)])
        raw = raw + bl_ref[layer : layer + 1]
        log_scale = jnp.tanh(raw)
        out_log[0] = log_scale
        logdet_ref[...] += jnp.sum(log_scale * own_mask, axis=0, keepdims=True)
        halves[1 - layer] = (target * jnp.exp(log_scale) + pltpu.roll(raw, LANE // 2, 1)) * image_mask
    for side in range(2):
        mine = pltpu.roll(halves[side], LANE - own, 1).T
        mine_s[step, :, side * cols : (side + 1) * cols] = mine[:16]

    @pl.when(step == samples - 1)
    def _():
        for s in range(samples):
            img_ref[:, s, :] = mine_s[s, :own]
        image = split(mine_s[...].reshape(samples * 16, 2 * cols))
        spectrum = dot3(image, (basis_ref[0], basis_ref[1]), ((1,), (0,)))
        blocks, _, lanes = col_ref.shape
        n_freq = lanes // (2 * samples)
        for d in range(blocks):
            chunk, offset = divmod(d * n_freq, LANE)
            total = jnp.zeros((16, LANE), F32)
            for part in range(2):
                for s in range(samples):
                    at = (part * samples + s) * n_freq
                    piece = spectrum[s * 16 : (s + 1) * 16, blk(part * (cols // LANE) + chunk)]
                    if at != offset:
                        piece = pltpu.roll(piece, (at - offset) % LANE, 1)
                    total = jnp.where((lane >= at) & (lane < at + n_freq), piece, total)
            col_ref[d] = total[:own, :lanes]


def backward_kernel(height, own, channels, reach, cells, r_ref, near_ref, loss_ref, wf_a, wf_b, wt_ref,
                    wl_a, wl_b, basis_ref, *rest):
    saved, lat_ref, out_ref, scratch = rest[:11], rest[11], rest[12], rest[13:]
    near_s, cot_s, dm, d0, dp, cpo_s, acc_mid, acc_last, acc_first, acc_bias = scratch
    step = pl.program_id(0)
    first = r_ref[0] * own
    lane = lane_ids(LANE)
    image_row = lane - own + first
    image_mask = ((lane < 3 * own) & (image_row >= 0) & (image_row < height)).astype(F32)
    raw_row = lane % (LANE // 2)
    own_mask = ((raw_row >= own) & (raw_row < 2 * own)).astype(F32)

    @pl.when(step == 0)
    def _():
        near_s[...] = jnp.zeros_like(near_s)
        blocks, span, lanes = near_ref.shape
        samples = pl.num_programs(0)
        n_freq = lanes // (2 * samples)
        per = LANE // n_freq
        for s in range(samples):
            for part in range(2):
                for chunk in range(blocks // per):
                    at = (part * samples + s) * n_freq
                    total = jnp.zeros((span, LANE), F32)
                    for i in range(per):
                        piece = near_ref[chunk * per + i]
                        if lanes < LANE:
                            piece = jnp.concatenate([piece] * (LANE // lanes), axis=1)
                        if at != i * n_freq:
                            piece = pltpu.roll(piece, (i * n_freq - at) % LANE, 1)
                        total = jnp.where((lane >= i * n_freq) & (lane < (i + 1) * n_freq), piece, total)
                    near_s[s * 32 : s * 32 + span, blk(part * (blocks // per) + chunk)] = total
        cot_s[...] = dot3((basis_ref[0], basis_ref[1]), split(near_s[...]), NT)
        for ref in (acc_mid, acc_last, acc_first, acc_bias):
            ref[...] = jnp.zeros_like(ref)

    def own_of(origin, block):
        row = origin + block * GROUP + lane // channels
        return ((row >= 0) & (row < own)).astype(F32)

    cols = lat_ref.shape[2]
    cots = []
    valid = (lane >= own - reach) & (lane < 2 * own + reach)
    shift = (own - reach + LANE - 32 * step) % LANE
    for side in range(2):
        cot = pltpu.roll(cot_s[side * cols : (side + 1) * cols, :], shift, 1)
        cots.append(jnp.where(valid, cot, 0.0))
    cond_one = saved[10][0]
    for layer, wf, wl in ((1, wf_b, wl_b), (0, wf_a, wl_a)):
        plan = PLAN[layer]
        h1, h2, s1, s2, log_ref = saved[5 * layer : 5 * layer + 5]
        cond = cond_one if layer == 1 else lat_ref[0, 0]
        target = lat_ref[0, 1 - layer]
        cot_new = cots[1 - layer]
        log_scale = log_ref[0]
        cot_log = cot_new * target * jnp.exp(log_scale) - 1.0 / cells
        scale_part = cot_log * (1.0 - log_scale * log_scale) * image_mask
        raw = scale_part + pltpu.roll(cot_new * image_mask, LANE // 2, 1)
        raw = raw.astype(BF).astype(F32)
        mine = raw * own_mask
        spread = jnp.concatenate([up(raw).astype(BF), raw.astype(BF), down(raw).astype(BF)], 1)
        spread_own = jnp.concatenate([up(mine).astype(BF), mine.astype(BF), down(mine).astype(BF)], 1)
        acc_last[layer] += dot(spread_own, h2[0], TN)
        acc_bias[layer, 2:3] += jnp.sum(mine, axis=0, keepdims=True)
        start2, count2 = plan["s2"]
        base1, _ = plan["h1"]
        for k in range(start2, start2 + count2):
            cot = dot(spread, wl[blk(k), :], NT) * s2[0, :, blk(k - start2)].astype(F32)
            plain = cot.astype(BF)
            cot = plain.astype(F32)
            parts = (up(cot).astype(BF), plain, down(cot).astype(BF))
            for ref, part in zip((dm, d0, dp), parts):
                ref[:, blk(k - start2)] = part
            local = k - base1
            if 0 <= local < 4:
                mask = own_of(plan["o2"], k)
                acc_bias[layer, 1:2] += jnp.sum(cot * mask, axis=0, keepdims=True)
                lhs = jnp.concatenate([part * mask.astype(BF) for part in parts], 1)
                acc_mid[layer] += dot(lhs, h1[0, :, blk(local, 2)], TN)
        high, low = split(taps(cond))
        start1, count1 = plan["s1"]
        for k in range(start1, start1 + count1):
            back = min(1, k - start2)
            cot = None
            for tap, ref in enumerate((dm, d0, dp)):
                term = dot(ref[:, blk(k - start2 - back, 1 + back)], wt_ref[layer, tap, (1 - back) * LANE :])
                cot = term if cot is None else cot + term
            plain = (cot * s1[0, :, blk(k - start1)].astype(F32)).astype(BF)
            cpo_s[:, blk(k - start1)] = plain
            if k - start1 < 4:
                mask = own_of(plan["o1"], k)
                mine = plain.astype(F32) * mask
                acc_bias[layer, 0:1] += jnp.sum(mine, axis=0, keepdims=True)
                mine = mine.astype(BF)
                acc_first[layer, :, blk(k - start1)] += dot(high, mine, TN) + dot(low, mine, TN)
        if layer == 1:
            full = cpo_s[:, blk(0, count1)]
            lanes = blk(start1, count1)
            terms = dot(full, wf[:LANE, lanes], NT) + dot(full, wf[2 * LANE :, lanes], NT)
            total = up(terms) + pltpu.roll(terms, LANE - SLOT, 1) * (lane < SLOT).astype(F32)
            total = jnp.where(lane < SLOT, total, 0.0)
            total = total + jnp.where(lane < SLOT, pltpu.roll(down(terms), LANE - 2 * SLOT, 1), 0.0)
            cots[1] = cots[1] + total

    @pl.when(step == pl.num_programs(0) - 1)
    def _():
        out_ref[...] = jnp.zeros_like(out_ref)
        layers = len(PLAN)
        side = slice(3 * channels, 4 * channels)
        fold_row = lax.broadcasted_iota(jnp.int32, (4 * LANE, channels), 0)
        fold_col = lax.broadcasted_iota(jnp.int32, (4 * LANE, channels), 1)
        fold = (fold_row % channels == fold_col).astype(F32)
        hi = lax.Precision.HIGHEST

        def folded(x):
            return jnp.dot(x, fold[: x.shape[1]], precision=hi, preferred_element_type=F32)

        def by_row(ref_value, groups, size, shift):
            shape = (groups * size, 4 * LANE)
            inner = lax.broadcasted_iota(jnp.int32, shape, 0) % size
            row = lax.broadcasted_iota(jnp.int32, shape, 1) // channels
            kept = jnp.where(row - inner == shift, ref_value, 0.0)
            return folded(jnp.sum(kept.reshape(groups, size, 4 * LANE), axis=1))

        for layer, plan in enumerate(PLAN):
            for dr in range(3):
                at = (layer * 3 + dr) * channels
                for dc in range(3):
                    total = None
                    for r in range(GROUP):
                        piece = acc_mid[layer, dc * LANE + r * channels : dc * LANE + (r + 1) * channels,
                                        (r + dr) * channels : (r + dr + 1) * channels]
                        total = piece if total is None else total + piece
                    out_ref[at : at + channels, dc * channels : (dc + 1) * channels] = total
                shift = dr - 1 - own - plan["o2"] - GROUP * plan["h2"][0]
                out_ref[at : at + 6, side] = by_row(acc_last[layer], 6, LANE // 2, shift)
                shift = 1 - dr - own - plan["o1"] - GROUP * plan["s1"][0]
                out_ref[at + 8 : at + 11, side] = by_row(
                    acc_first[layer, : 3 * SLOT], 3, SLOT, shift)
            at = layer * 3 * channels + 16
            out_ref[at : at + 2, side] = folded(acc_bias[layer, 0:2])
            bias = acc_bias[layer, 2:3]
            pick = lane_ids(channels)
            low = jnp.sum(jnp.where(lane < LANE // 2, bias, 0.0), axis=1, keepdims=True)
            top = jnp.sum(jnp.where(lane >= LANE // 2, bias, 0.0), axis=1, keepdims=True)
            out_ref[at + 2 : at + 3, side] = jnp.where(
                pick == 0, low, jnp.where(pick == 1, top, jnp.where(pick == 2, loss_ref[...], 0.0)))


def prepare(own, first_ref, mid_ref, last_ref, bf_ref, bm_ref, bl_ref, wf_a, wf_b, wm_ref, wt_ref, wl_a, wl_b,
            bf_out, bm_out, bl_out):
    channels = mid_ref.shape[2]
    lane = lane_ids(LANE)

    def tiled(x):
        return jnp.concatenate([x] * GROUP, axis=1)

    bf_out[...] = tiled(bf_ref[...])
    bm_out[...] = tiled(bm_ref[...])
    bl_out[...] = jnp.where(lane < LANE // 2, bl_ref[:, 0:1], bl_ref[:, 1:2])
    spread = (lax.broadcasted_iota(jnp.int32, (channels, LANE), 0) == lane % channels).astype(BF)
    parts = lax.broadcasted_iota(jnp.int32, (8, 3 * LANE), 0)
    parts = (parts == lax.broadcasted_iota(jnp.int32, (8, 3 * LANE), 1) // (LANE // 2)).astype(BF)
    wide_lane = lane_ids(3 * LANE) % (LANE // 2)
    edge = lax.broadcasted_iota(jnp.int32, (SLOT, LANE), 0)
    for layer, (wf, wl) in enumerate(((wf_a, wl_a), (wf_b, wl_b))):
        plan = PLAN[layer]
        rows = tiled(first_ref[layer])
        for k in range(plan["n1"]):
            row = k * GROUP + lane // channels + plan["o1"] + own - 1
            pieces = []
            for dc in range(3):
                total = jnp.zeros((SLOT, LANE), F32)
                for dr in range(3):
                    hit = (edge == row + dr) & (edge < 3 * own)
                    total = total + jnp.where(hit, rows[3 * dr + dc : 3 * dr + dc + 1], 0.0)
                pieces.append(total)
            pieces.append(jnp.zeros((LANE - 3 * SLOT, LANE), F32))
            high, low = split(jnp.concatenate(pieces, axis=0))
            wf[:LANE, blk(k)] = high
            wf[LANE : 2 * LANE, blk(k)] = high
            wf[2 * LANE :, blk(k)] = low
        for dc in range(3):
            taps_t = [dot(mid_ref[layer, 3 * dr + dc], spread, TN) for dr in range(3)]
            band = []
            for row in range(2 * GROUP):
                total = jnp.zeros((channels, LANE), F32)
                for dr in range(3):
                    if 0 <= row - dr < GROUP:
                        total = total + jnp.where(lane // channels == row - dr, taps_t[dr], 0.0)
                band.append(total)
            top = jnp.concatenate(band[:GROUP], axis=0)
            low = jnp.concatenate(band[GROUP:], axis=0)
            wm_ref[layer, dc, :LANE] = top.astype(BF)
            wm_ref[layer, dc, LANE:] = low.astype(BF)
            wt_ref[layer, dc, :LANE] = low.T.astype(BF)
            wt_ref[layer, dc, LANE:] = top.T.astype(BF)
        columns = [dot(last_ref[layer, dr], parts, TN) for dr in range(3)]
        for row in range(plan["n2"] * GROUP):
            total = jnp.zeros((channels, 3 * LANE), F32)
            for dr in range(3):
                hit = (wide_lane == row + own + 1 - dr + plan["o2"]) & (wide_lane < 3 * own)
                total = total + jnp.where(hit, columns[dr], 0.0)
            wl[row * channels : (row + 1) * channels, :] = total.astype(BF)


def butterfly(value, axes=("grp", "rows")):
    for axis in axes:
        count = lax.axis_size(axis)
        hop = 1
        while hop < count:
            value = value + lax.ppermute(value, axis, [(i, i ^ hop) for i in range(count)])
            hop *= 2
    return value


def grid_kernel(n_freq, pad_freq, height, img_width, r_ref, u_ref, v_ref, obs_ref, w_ref, out_ref, const_ref,
                u_s, c_s, sign_s):
    share = u_s.shape[0]
    start = pl.multiple_of(r_ref[1] * share, share)
    half = img_width // 2
    u = u_ref[pl.ds(start, share), :]
    v = v_ref[pl.ds(start, share), :]
    mirror = v > half
    v_fold = jnp.where(mirror, img_width - v, v)
    col = v_fold - r_ref[0] * n_freq
    col = jnp.where((col < 0) | (col >= n_freq), pad_freq, col)
    u_s[...] = jnp.where(mirror & (u > 0), height - u, u)
    c_s[...] = jnp.where(v_fold == half, n_freq, col)
    sign_s[...] = jnp.where(mirror, -1.0, 1.0)
    out_ref[...] = jnp.zeros_like(out_ref)
    ids = lax.broadcasted_iota(jnp.int32, (16, LANE), 0).astype(jnp.int16)
    slots = lax.broadcasted_iota(jnp.int32, (pad_freq, LANE), 0)
    one = jnp.ones((16, LANE), BF)
    zero = jnp.zeros((16, LANE), BF)
    group = 16

    def one_step(j, total):
        hots, values = [], []
        for q in range(group):
            row = pl.ds(j * group + q, 1)
            u_row = jnp.broadcast_to(u_s[row, :], (16, LANE)).astype(jnp.int16)
            hots.append(jnp.concatenate(
                [jnp.where(ids + jnp.int16(16 * g) == u_row, one, zero) for g in range(height // 16)], axis=0))
            c_hot = slots == c_s[row, :]
            lanes = pl.ds(pl.multiple_of((start + j * group + q) * LANE, LANE), LANE)
            w = w_ref[pl.ds(start + j * group + q, 1), :]
            o_re, o_im = obs_ref[0:1, lanes], obs_ref[1:2, lanes]
            total = total + w * (o_re * o_re + o_im * o_im)
            parts = []
            for full in (w, w * o_re, w * o_im * sign_s[row, :]):
                high = full.astype(BF).astype(F32)
                parts += [jnp.where(c_hot, high, 0.0), jnp.where(c_hot, full - high, 0.0)]
            values.append(jnp.concatenate(parts, axis=0).astype(BF))
        out_ref[...] += dot(jnp.concatenate(hots, axis=1), jnp.concatenate(values, axis=1), NT)
        return total

    total = lax.fori_loop(0, share // group, one_step, jnp.zeros((1, LANE), F32))
    const_ref[...] = jnp.sum(total, axis=(0, 1), keepdims=True)


def slot_count(n_freq):
    return 8 * ((n_freq + 8) // 8)


def lane_selection(samples, n_freq):
    pad_freq = slot_count(n_freq)
    lanes = 2 * samples * n_freq
    sel = np.zeros((2, 3, 6 * pad_freq, lanes), np.float32)
    for special in range(2):
        for lane in range(lanes):
            part, freq = lane // (samples * n_freq), lane % n_freq
            lone = special == 1 and freq == 0
            slot = n_freq if lone and part == 1 else freq
            fields = (0, 1, 2) if lone else (0, 1 + part, None)
            for out_id, field in enumerate(fields):
                if field is not None:
                    for piece in range(2):
                        sel[special, out_id, (2 * field + piece) * pad_freq + slot, lane] = 1.0
    return sel


def gridded(vis_u, vis_v, observed, vis_weight, height, img_width, n_rows, n_grp):
    n_freq = img_width // 2 // n_rows
    pad_freq = slot_count(n_freq)
    rows = vis_u.shape[0] // LANE
    share = rows // n_grp
    vmem = pl.BlockSpec(memory_space=pltpu.VMEM)
    where = jnp.stack([lax.axis_index("rows"), lax.axis_index("grp")]).astype(jnp.int32)
    return pl.pallas_call(
        functools.partial(grid_kernel, n_freq, pad_freq, height, img_width),
        out_shape=(jax.ShapeDtypeStruct((height, 6 * pad_freq), F32),
                   jax.ShapeDtypeStruct((1, 1), F32)),
        in_specs=[pl.BlockSpec(memory_space=pltpu.SMEM)] + [vmem] * 4,
        out_specs=(vmem, vmem),
        scratch_shapes=[pltpu.VMEM((share, LANE), jnp.int32), pltpu.VMEM((share, LANE), jnp.int32),
                        pltpu.VMEM((share, LANE), F32)],
        compiler_params=pltpu.CompilerParams(vmem_limit_bytes=24 * 2**20),
        cost_estimate=pl.CostEstimate(flops=2 * height * 256 * share * LANE * 4,
                                      bytes_accessed=24 * share * LANE, transcendentals=0),
    )(where, vis_u.reshape(rows, LANE), vis_v.reshape(rows, LANE), observed, vis_weight.reshape(rows, LANE))


def column_basis(img_width):
    cols = np.arange(img_width)
    freq = np.arange(img_width // 2)
    angle = 2.0 * np.pi * ((cols[:, None] * freq[None, :]) % img_width) / img_width
    re, im = np.cos(angle), -np.sin(angle)
    im[:, 0] = 1.0 - 2.0 * (cols % 2)
    return np.concatenate([re, im], axis=1).astype(np.float32)


def spectral_kernel(scale, factor, half, n_freq, own, reach, r_ref, z_ref, cs_ref, grid_ref, sel_ref, near_ref,
                    data_ref, near_s):
    height, lanes = z_ref.shape
    lane = lax.broadcasted_iota(jnp.int32, (1, lanes), 1)
    lone = ((lane % n_freq) == 0) & (r_ref[0] == 0)
    sign = jnp.where(lane < half, 1.0, -1.0)
    hi = lax.Precision.HIGHEST
    z = z_ref[...] * scale
    a = jnp.dot(cs_ref[0], z, precision=hi, preferred_element_type=jnp.float32)
    b = jnp.dot(cs_ref[1], z, precision=hi, preferred_element_type=jnp.float32)
    kind = jnp.where(r_ref[0] == 0, 1, 0)
    w, t1, t2 = [
        jnp.dot(grid_ref[...], sel_ref[kind, i], precision=hi, preferred_element_type=F32) for i in range(3)
    ]

    def swap(x):
        return jnp.concatenate([x[:, half:], x[:, :half]], axis=1)

    x = jnp.where(lone, a, a + sign * swap(b))
    p = w * x - t1
    q = jnp.where(lone, w * b + t2, -sign * swap(p))
    b_lone = jnp.where(lone, b, 0.0)
    terms = w * (x * x + b_lone * b_lone) - 2.0 * (x * t1 - b_lone * t2)
    data_ref[...] = jnp.sum(terms, axis=(0, 1), keepdims=True)
    near = jnp.dot(cs_ref[2], p, precision=hi, preferred_element_type=jnp.float32)
    near = near + jnp.dot(cs_ref[3], q, precision=hi, preferred_element_type=jnp.float32)
    near_s[...] = jnp.zeros_like(near_s)
    near_s[8 : 8 + height, :] = near * (factor * scale)
    for d in range(near_ref.shape[0]):
        near_ref[d] = near_s[8 + d * own - reach : 8 + (d + 1) * own + reach, :]


def spectral(z, grid, scale, factor, samples, own, reach):
    height, lanes = z.shape
    ids = np.arange(height)
    angle = 2.0 * np.pi * ((ids[:, None] * ids[None, :]) % height) / height
    cs = np.stack([np.cos(angle), np.sin(angle), np.cos(angle), np.sin(angle)]).astype(np.float32)
    vmem = pl.BlockSpec(memory_space=pltpu.VMEM)
    return pl.pallas_call(
        functools.partial(spectral_kernel, scale, factor, lanes // 2, lanes // (2 * samples), own, reach),
        out_shape=(jax.ShapeDtypeStruct((height // own, own + 2 * reach, lanes), F32),
                   jax.ShapeDtypeStruct((1, 1), F32)),
        in_specs=[pl.BlockSpec(memory_space=pltpu.SMEM)] + [vmem] * 4,
        out_specs=(vmem, vmem),
        scratch_shapes=[pltpu.VMEM((height + 16, lanes), F32)],
        compiler_params=pltpu.CompilerParams(vmem_limit_bytes=24 * 2**20),
    )(lax.axis_index("rows")[None].astype(jnp.int32), z, jnp.asarray(cs), grid,
      jnp.asarray(lane_selection(samples, lanes // (2 * samples))))


def body(
    latent, w_first, b_first, w_mid, b_mid, w_last, b_last, vis_u, vis_v, observed, vis_weight
):
    samples, row_count, img_width = latent.shape
    half_cols = img_width // 2
    n_rows = lax.axis_size("rows")
    n_grp = lax.axis_size("grp")
    height = row_count * n_rows
    batch_size = samples * n_grp
    layers = w_first.shape[0]
    vis_total = vis_u.shape[0]
    cells = height * img_width
    channels = w_mid.shape[2]
    half = half_cols
    n_freq = img_width // 2 // n_rows
    forward = [(i, i + 1) for i in range(n_rows - 1)]
    backward = [(target, source) for source, target in forward]
    low = lax.ppermute(latent, "rows", forward)
    high = lax.ppermute(latent, "rows", backward)
    grid, obs_const = gridded(
        vis_u, vis_v, observed, vis_weight, height, img_width, n_rows, n_grp
    )
    low, high, grid = lax.optimization_barrier((low, high, grid))
    grid = butterfly(grid, ("grp",))
    pieces = [value.transpose(1, 0, 2) for value in (low, latent, high)]
    last = jnp.pad(w_last.reshape(layers, 3, 6, channels), ((0, 0), (0, 0), (0, 2), (0, 0)))
    weights = (w_first.reshape(layers, 9, channels), w_mid, last, b_first, b_mid, b_last)
    basis_np = column_basis(img_width)
    basis_high = basis_np.astype(BF)
    basis_low = (basis_np - basis_high.astype(np.float32)).astype(BF)
    basis = jnp.asarray(np.stack([basis_high, basis_low]))
    index = lax.axis_index("rows")[None].astype(jnp.int32)
    smem = pl.BlockSpec(memory_space=pltpu.SMEM)

    def whole(value):
        rank = len(value.shape)
        return pl.BlockSpec(value.shape, lambda s: (0,) * rank)

    def per_sample(*shape):
        rank = len(shape)
        return pl.BlockSpec((1,) + shape, lambda s: (s,) + (0,) * rank)

    saved_shapes = []
    for plan in PLAN:
        for key, kind in (("h1", BF), ("h2", BF), ("s1", BF), ("s2", BF)):
            saved_shapes.append(((half, plan[key][1] * LANE), kind))
        saved_shapes.append(((half, LANE), F32))
    saved_shapes.append(((half, LANE), F32))
    saved_shapes.append(((2, half, LANE), F32))
    saved_specs = [per_sample(*shape) for shape, kind in saved_shapes]
    saved_types = [jax.ShapeDtypeStruct((samples,) + shape, kind) for shape, kind in saved_shapes]
    weights = weights + (basis,)
    bands = [((3 * LANE, plan["n1"] * LANE), BF) for plan in PLAN]
    bands += [((layers, 3, 2 * LANE, LANE), BF)]
    bands += [((plan["n2"] * LANE, 3 * LANE), BF) for plan in PLAN]
    bands = [jax.ShapeDtypeStruct(shape, kind) for shape, kind in bands]
    max1 = max(plan["n1"] for plan in PLAN) * LANE
    max2 = max(plan["n2"] for plan in PLAN) * LANE
    params = pltpu.CompilerParams(vmem_limit_bytes=58 * 2**20)
    image_out, columns, logdet, wf_a, wf_b, wt, wl_a, wl_b, *saved = pl.pallas_call(
        functools.partial(forward_kernel, height, row_count, channels),
        grid=(samples,),
        out_shape=(
            jax.ShapeDtypeStruct((row_count, samples, img_width), F32),
            jax.ShapeDtypeStruct((n_rows, row_count, 2 * samples * n_freq), F32),
            jax.ShapeDtypeStruct((1, LANE), F32),
            *bands,
            *saved_types,
        ),
        in_specs=[smem] + [whole(value) for value in (*pieces, *weights)],
        out_specs=(
            pl.BlockSpec((row_count, samples, img_width), lambda s: (0, 0, 0)),
            pl.BlockSpec((n_rows, row_count, 2 * samples * n_freq), lambda s: (0, 0, 0)),
            pl.BlockSpec((1, LANE), lambda s: (0, 0)),
            *[whole(band) for band in bands],
            *saved_specs,
        ),
        scratch_shapes=[pltpu.VMEM((layers, 3, 2 * LANE, LANE), BF)]
        + [pltpu.VMEM((layers, LANE), F32)] * 3
        + [pltpu.VMEM((half, max1), BF)] * 3
        + [
            pltpu.VMEM((half, max2), BF),
            pltpu.VMEM((LANE, img_width), F32),
            pltpu.VMEM((samples, 2, half, LANE), F32),
            pltpu.VMEM((samples, 16, img_width), F32),
        ],
        compiler_params=params,
    )(index, *pieces, *weights)
    image_out = image_out.transpose(1, 0, 2)
    logdet = jnp.sum(logdet)
    norm_scale = 1.0 / math.sqrt(height * img_width)
    reach = 6
    factor = 2.0 / (vis_total * batch_size)
    columns = lax.all_to_all(columns, "rows", 0, 0, tiled=True)
    near, data_sum = spectral(
        columns.reshape(height, 2 * samples * n_freq), grid, norm_scale, factor, samples, row_count, reach
    )
    near = lax.all_to_all(near, "rows", 0, 0, tiled=True)
    span = row_count + 2 * reach
    data_part = (data_sum[0, 0] + batch_size * obs_const[0, 0] / n_rows) / vis_total
    loss_part = (data_part - logdet / (height * img_width)) / batch_size
    out_rows = layers * 3 * channels
    weights = (wf_a, wf_b, wt, wl_a, wl_b, basis)
    flat = pl.pallas_call(
        functools.partial(
            backward_kernel, height, row_count, channels, reach, batch_size * cells
        ),
        grid=(samples,),
        out_shape=jax.ShapeDtypeStruct((out_rows, LANE), F32),
        in_specs=[smem, whole(near), pl.BlockSpec((1, 1), lambda s: (0, 0))]
        + [whole(value) for value in weights] + saved_specs,
        out_specs=pl.BlockSpec((out_rows, LANE), lambda s: (0, 0)),
        scratch_shapes=[
            pltpu.VMEM((LANE, img_width), F32),
            pltpu.VMEM((img_width, LANE), F32),
            *[pltpu.VMEM((half, max2), BF)] * 3,
            pltpu.VMEM((half, max1), BF),
            pltpu.VMEM((layers, 3 * LANE, 2 * LANE), F32),
            pltpu.VMEM((layers, 3 * LANE, 4 * LANE), F32),
            pltpu.VMEM((layers, LANE, 4 * LANE), F32),
            pltpu.VMEM((layers, 8, LANE), F32),
        ],
        compiler_params=params,
    )(index, near, loss_part.reshape(1, 1), *weights, *saved)
    flat = butterfly(flat)
    main = flat[:, : 3 * channels]
    main = main.reshape(layers, 3, channels, 3, channels).transpose(0, 1, 3, 2, 4)
    rest = flat[:, 3 * channels :].reshape(layers, 3, channels, channels)
    final_grads = [
        rest[:, :, 8:11].reshape(layers, 9, channels, 1),
        main.reshape(layers, 9, channels, channels),
        rest[:, :, :6].reshape(layers, 9, 2, channels),
        rest[:, 0, 16],
        rest[:, 0, 17],
        rest[:, 0, 18, :2],
    ]
    loss = rest[0, 0, 18, 2]
    return (
        image_out,
        loss,
        final_grads[0],
        final_grads[1],
        final_grads[2],
        final_grads[3],
        final_grads[4],
        final_grads[5],
    )


def solution(mesh):
    in_specs = (P("grp", "rows", None), P(), P(), P(), P(), P(), P(), P(), P(), P(), P())
    out_specs = (P("grp", "rows", None), P(), P(), P(), P(), P(), P(), P())
    return jax.shard_map(body, mesh=mesh, in_specs=in_specs, out_specs=out_specs, check_vma=False)
```

time: 151 us -> 130 us (0.86)
  local copies, waits for them, and re-layouts: 25.8 us -> 10.5 us
  waiting for transfers between devices: 24.6 us -> 31.1 us
  Pallas kernels: 67.7 us -> 61.6 us
  starting transfers between devices: 25.5 us -> 22.3 us
  other arithmetic: 3.33 us -> 1.66 us
    reshape x11 -> x2, local copies, waits for them, and re-layouts: 9.81 us -> 0.61 us  [the longest x1 0.61 us: body(): w_first.reshape(layers, 9, channels)]
    pallas_call x2 -> x1, Pallas kernels: 16 us -> 7.29 us  [gridded(): pl.pallas_call(functools.partial(grid_kernel, n_freq, pad_freq, height, i...]
    all_to_all x1, waiting for transfers between devices: 0.01 us -> 6.24 us  [body(): columns = lax.all_to_all(columns, 'rows', 0, 0, tiled=True)]
    unnamed x44 -> x30, local copies, waits for them, and re-layouts: 9.84 us -> 6.51 us
    all_to_all x1, starting transfers between devices: 6.91 us -> 3.7 us  [body(): near = lax.all_to_all(near, 'rows', 0, 0, tiled=True)]
    pallas_call x1, Pallas kernels: 23.1 us -> 25.7 us  [body(): pl.pallas_call(functools.partial(forward_kernel, height, row_count, chann...]
    ppermute x5 -> x6, waiting for transfers between devices: 19.1 us -> 19.6 us  [butterfly(): lax.ppermute(value, axis, [(i, i ^ hop) for i in range(count)])]
    ppermute x5 -> x6, starting transfers between devices: 4.33 us -> 4.42 us  [butterfly(): lax.ppermute(value, axis, [(i, i ^ hop) for i in range(count)])]
  transfers between devices with their start and end apart: 9 -> 10, of which waited for: 6 -> 8; matrix products, arithmetic and copies ran while one was open for 5% -> 1% of each run, Pallas kernels for 11% -> 6%
where the time goes in v1:
time: 130 us
  Pallas kernels  61.6 us (47%)
  waiting for transfers between devices  31.1 us (24%)
  starting transfers between devices  22.3 us (17%)
  local copies, waits for them, and re-layouts  10.5 us (8%)
  between operations  2.78 us (2%)
  other arithmetic  1.66 us (1%)
    pallas_call x1, Pallas kernels, body(): pl.pallas_call(functools.partial(backward_kernel, height, row_count, chan...  25.9 us
    pallas_call x1, Pallas kernels, body(): pl.pallas_call(functools.partial(forward_kernel, height, row_count, chann...  25.7 us
    ppermute x6, waiting for transfers between devices, butterfly(): lax.ppermute(value, axis, [(i, i ^ hop) for i in range(count)])  19.6 us
    all_to_all x1, starting transfers between devices, body(): columns = lax.all_to_all(columns, 'rows', 0, 0, tiled=True)  8.03 us
    pallas_call x1, Pallas kernels, gridded(): pl.pallas_call(functools.partial(grid_kernel, n_freq, pad_freq, height, i...  7.29 us
    unnamed x30, local copies, waits for them, and re-layouts  6.51 us
    all_to_all x1, waiting for transfers between devices, body(): columns = lax.all_to_all(columns, 'rows', 0, 0, tiled=True)  6.24 us
    all_to_all x1, waiting for transfers between devices, body(): near = lax.all_to_all(near, 'rows', 0, 0, tiled=True)  5.3 us
  transfers between devices with their start and end apart: 10, of which 8 were waited for; matrix products, arithmetic and copies ran while one was open for 1% of the time, Pallas kernels for 6%

profile of v1, /device:TPU:0, one launch (start us, length us, event | category | flops | bytes accessed | tf_op | source)
XLA Modules:
  0.0 129.9 jit_solution(3149406912671996329)
XLA Ops:
  0.6 4.8 %collective-permute-start = (f32[4,12,512]{2,0,1:T(4,128)}, f32[4,12,512]{2,0,1:T(4,128)S(1)}, u32[]{:S(2)}, u32[]{:S(2)}) collective-permute-start(f32[4,12,512]{2,0,1:T(4,128)} %param.14), channel_id=1, source_target_pairs={{0,2},{2,4},{4,6},{6,8},{8,10},{10,12},{12,14},{14,16},{16,18},{18... | collective-permute-start | bytes 294920 | tf_op jit(solution)/shard_map/ppermute | solution.py:547
  5.5 1.3 collective-permute-start.1
  6.9 1.0 copy-done.2
  7.9 0.9 copy-done.3
  8.9 0.9 copy-done.4
  9.8 0.9 copy-done.5
  10.8 7.3 %shard_map.197 = (f32[192,144]{1,0:T(8,128)S(1)}, f32[1,1]{1,0:T(1,128)}) custom-call(s32[2]{0:T(128)S(1)} %pad_add_fusion.r_ref, s32[512,128]{1,0:T(8,128)S(1)} %bitcast.31, s32[512,128]{1,0:T(8,128)S(1)} %bitcast.32, f32[2,65536]{1,0:T(2,128)S(1)} %copy-done.2, f32[512,128]{1,0:T(8,128)S(1)} %bitcast.33), custom_call_target="tpu_custom_call" | custom-call | flops 12884901888 | bytes 786432 | tf_op jit(solution)/shard_map/pallas_call | solution.py:457
  18.1 0.6 copy.40.first_ref
  18.7 0.6 pad.4.last_ref
  19.3 0.6 copy-done.7
  20.0 25.7 %shard_map.198 = (f32[12,4,512]{2,1,0:T(4,128)}, f32[16,12,128]{2,1,0:T(8,128)}, f32[1,128]{1,0:T(1,128)}, bf16[384,1024]{1,0:T(8,128)(2,1)}, bf16[384,896]{1,0:...) custom-call(s32[1]{0:T(128)} %bitcast.r_ref, ...), custom_call_target="tpu_custom_call" | custom-call | tf_op jit(solution)/shard_map/pallas_call | solution.py:589
  45.7 8.0 %all-to-all-start = ((f32[16,12,128]{2,1,0:T(8,128)}), f32[16,12,128]{2,1,0:T(8,128)S(1)}, u32[]{:S(2)}, u32[]{:S(2)}) async-start(f32[16,12,128]{2,1,0:T(8,128)} %get-tuple-element.39), calls=%async_computation | async-start | bytes 262144 | tf_op jit(solution)/shard_map/all_to_all | solution.py:623
  53.9 1.4 %collective-permute-done.2 = f32[192,144]{1,0:T(8,128)S(1)} collective-permute-done((f32[192,144]{1,0:T(8,128)S(1)}, f32[192,144]{1,0:T(8,128)S(1)}, u32[]{:S(2)}, u32[]{:S(2)}) %collective-permute-start.2) | collective-permute-done | bytes 110624 | tf_op jit(solution)/shard_map/ppermute | solution.py:379
  55.3 6.2 %all-to-all-done = f32[16,12,128]{2,1,0:T(8,128)S(1)} async-done(((f32[16,12,128]{2,1,0:T(8,128)}), f32[16,12,128]{2,1,0:T(8,128)S(1)}, u32[]{:S(2)}, u32[]{:S(2)}) %all-to-all-start) | async-done | bytes 98336 | tf_op jit(solution)/shard_map/all_to_all | solution.py:623
  61.6 2.7 %shard_map.199 = (f32[16,24,128]{2,1,0:T(8,128)}, f32[1,1]{1,0:T(1,128)}) custom-call(s32[1]{0:T(128)} %bitcast.r_ref, f32[192,128]{1,0:T(8,128)S(1)} %reshape.62.z_ref, f32[4,192,192]{2,1,0:T(8,128)S(1)} %copy-done, f32[192,144]{1,0:T(8,128)S(1)} %add.24.grid_ref, f32[2,3,144,128]{3,2,1,0:T(8,128)S(1)} %copy-done.1), custom_call_target="tpu_custom_call" | custom-call | tf_op jit(solution)/shard_map/pallas_call | solution.py:518
  64.3 3.7 %all-to-all-start.1 = ((f32[16,24,128]{2,1,0:T(8,128)}), f32[16,24,128]{2,1,0:T(8,128)S(1)}, u32[]{:S(2)}, u32[]{:S(2)}) async-start(f32[16,24,128]{2,1,0:T(8,128)} %get-tuple-element.41), calls=%async_computation.1 | async-start | bytes 393216 | tf_op jit(solution)/shard_map/all_to_all | solution.py:627
  70.5 5.3 %all-to-all-done.1.near_ref = f32[16,24,128]{2,1,0:T(8,128)S(1)} async-done(((f32[16,24,128]{2,1,0:T(8,128)}), f32[16,24,128]{2,1,0:T(8,128)S(1)}, u32[]{:S(2)}, u32[]{:S(2)}) %all-to-all-start.1) | async-done | bytes 196640 | tf_op jit(solution)/shard_map/all_to_all | solution.py:627
  75.8 0.7 copy-done.6
  76.5 25.9 %shard_map.200 = f32[192,128]{1,0:T(8,128)} custom-call(s32[1]{0:T(128)} %bitcast.r_ref, f32[16,24,128]{2,1,0:T(8,128)} %copy-done.6, f32[1,1]{1,0:T(1,128)} %bitcast.12.loss_ref, bf16[384,1024]{1,0:T(8,128)(2,1)} %get-tuple-element.45.wf_a, bf16[384,896]{1,0:T(8,128)(2,1)} %get-tuple-element.46.wf_b, bf16[2,3,256,128]{3,2,1,0:T(8,128)(2,1)} %get-tuple-element.47.wt_ref, ...), custom_call_target="tpu_custom_call" | custom-call | tf_op jit(solution)/shard_map/pallas_call | solution.py:633
  102.5 1.5 %collective-permute-done.3 = f32[192,128]{1,0:T(8,128)S(1)} collective-permute-done((f32[192,128]{1,0:T(8,128)}, f32[192,128]{1,0:T(8,128)S(1)}, u32[]{:S(2)}, u32[]{:S(2)}) %collective-permute-start.3) | collective-permute-done | bytes 98336 | tf_op jit(solution)/shard_map/ppermute | solution.py:379
  104.0 0.9 add.26
  104.9 1.4 %collective-permute-start.4 = (f32[192,128]{1,0:T(8,128)S(1)}, f32[192,128]{1,0:T(8,128)S(1)}, u32[]{:S(2)}, u32[]{:S(2)}) collective-permute-start(f32[192,128]{1,0:T(8,128)S(1)} %add.26), channel_id=1, source_target_pairs={{0,2},{2,0},{4,6},{6,4},{8,10},{10,8},{12,14},{14,12},{16,18},{18,... | collective-permute-start | bytes 294920 | tf_op jit(solution)/shard_map/ppermute | solution.py:379
  106.3 3.5 %collective-permute-done.4 = f32[192,128]{1,0:T(8,128)S(1)} collective-permute-done((f32[192,128]{1,0:T(8,128)S(1)}, f32[192,128]{1,0:T(8,128)S(1)}, u32[]{:S(2)}, u32[]{:S(2)}) %collective-permute-start.4) | collective-permute-done | bytes 98336 | tf_op jit(solution)/shard_map/ppermute | solution.py:379
  109.8 0.9 collective-permute-start.5
  110.7 3.8 %collective-permute-done.5 = f32[192,128]{1,0:T(8,128)S(1)} collective-permute-done((f32[192,128]{1,0:T(8,128)S(1)}, f32[192,128]{1,0:T(8,128)S(1)}, u32[]{:S(2)}, u32[]{:S(2)}) %collective-permute-start.5) | collective-permute-done | bytes 98336 | tf_op jit(solution)/shard_map/ppermute | solution.py:379
  114.5 0.9 collective-permute-start.6
  115.4 3.8 %collective-permute-done.6 = f32[192,128]{1,0:T(8,128)S(1)} collective-permute-done((f32[192,128]{1,0:T(8,128)S(1)}, f32[192,128]{1,0:T(8,128)S(1)}, u32[]{:S(2)}, u32[]{:S(2)}) %collective-permute-start.6) | collective-permute-done | bytes 98336 | tf_op jit(solution)/shard_map/ppermute | solution.py:379
  119.2 1.1 collective-permute-start.7
  120.4 5.5 %collective-permute-done.7 = f32[192,128]{1,0:T(8,128)S(1)} collective-permute-done((f32[192,128]{1,0:T(8,128)S(1)}, f32[192,128]{1,0:T(8,128)S(1)}, u32[]{:S(2)}, u32[]{:S(2)}) %collective-permute-start.7) | collective-permute-done | bytes 98336 | tf_op jit(solution)/shard_map/ppermute | solution.py:379
  127.7 0.6 copy.47
  128.4 0.6 copy.48
  129.2 0.7 copy.42
  (42 shorter events, 3.0 us)
Async XLA Ops:
  0.6 18.7 %collective-permute-start = (f32[4,12,512]{2,0,1:T(4,128)}, f32[4,12,512]{2,0,1:T(4,128)S(1)}, u32[]{:S(2)}, u32[]{:S(2)}) collective-permute-start(f32[4,12,512]{2,0,1:T(4,128)} %param.14), channel_id=1, source_target_pairs={{0,2},{2,4},{4,6},{6,8},{8,10},{10,12},{12,14},{14,16},{16,18},{18... | collective-permute-start | bytes 294920 | tf_op jit(solution)/shard_map/ppermute | solution.py:547
  5.5 13.8 %collective-permute-start.1 = (f32[4,12,512]{2,0,1:T(4,128)}, f32[4,12,512]{2,0,1:T(4,128)S(1)}, u32[]{:S(2)}, u32[]{:S(2)}) collective-permute-start(f32[4,12,512]{2,0,1:T(4,128)} %param.14), channel_id=1, source_target_pairs={{2,0},{4,2},{6,4},{8,6},{10,8},{12,10},{14,12},{16,14},{18,16},{20... | collective-permute-start | bytes 294920 | tf_op jit(solution)/shard_map/ppermute | solution.py:548
  6.9 1.0 copy-start.2
  7.9 0.9 copy-start.3
  8.9 0.9 copy-start.4
  9.8 0.9 copy-start.5
  10.8 7.3 %copy-start.9 = (f32[2,9,32,1]{2,3,1,0:T(1,128)S(1)}, f32[2,9,32,1]{2,3,1,0:T(1,128)}, u32[]{:S(2)}) copy-start(f32[2,9,32,1]{2,3,1,0:T(1,128)} %param.15) | copy-start | bytes 6916
  10.8 7.9 %copy-start.10 = (bf16[2,9,2,32]{3,2,1,0:T(2,128)(2,1)S(1)}, bf16[2,9,2,32]{3,2,1,0:T(2,128)(2,1)}, u32[]{:S(2)}) copy-start(bf16[2,9,2,32]{3,2,1,0:T(2,128)(2,1)} %param.19) | copy-start | bytes 6916
  19.3 42.3 %copy-start = (f32[4,192,192]{2,1,0:T(8,128)S(1)}, f32[4,192,192]{2,1,0:T(8,128)}, u32[]{:S(2)}) copy-start(f32[4,192,192]{2,1,0:T(8,128)} %constant.35.clone.cs_ref) | copy-start | bytes 1769476
  19.3 42.3 %copy-start.1 = (f32[2,3,144,128]{3,2,1,0:T(8,128)S(1)}, f32[2,3,144,128]{3,2,1,0:T(8,128)}, u32[]{:S(2)}) copy-start(f32[2,3,144,128]{3,2,1,0:T(8,128)} %constant.36.clone.sel_ref) | copy-start | bytes 1327108
  19.3 0.6 copy-start.7
  19.3 0.7 copy-start.8
  45.7 15.8 %all-to-all-start = ((f32[16,12,128]{2,1,0:T(8,128)}), f32[16,12,128]{2,1,0:T(8,128)S(1)}, u32[]{:S(2)}, u32[]{:S(2)}) async-start(f32[16,12,128]{2,1,0:T(8,128)} %get-tuple-element.39), calls=%async_computation | async-start | bytes 262144 | tf_op jit(solution)/shard_map/all_to_all | solution.py:623
  53.8 14.8 %copy-start.11 = (f32[1,128]{1,0:T(1,128)S(1)}, f32[1,128]{1,0:T(1,128)}, u32[]{:S(2)}) copy-start(f32[1,128]{1,0:T(1,128)} %get-tuple-element.44) | copy-start | bytes 1540
  53.8 1.5 %collective-permute-start.2 = (f32[192,144]{1,0:T(8,128)S(1)}, f32[192,144]{1,0:T(8,128)S(1)}, u32[]{:S(2)}, u32[]{:S(2)}) collective-permute-start(f32[192,144]{1,0:T(8,128)S(1)} %get-tuple-element.40), channel_id=1, source_target_pairs={{0,1},{1,0},{2,3},{3,2},{4,5},{5,4},{6,7},{7,6},{8,9},{9,8},{10,11... | collective-permute-start | bytes 331784 | tf_op jit(solution)/shard_map/ppermute | solution.py:379
  64.3 11.6 %all-to-all-start.1 = ((f32[16,24,128]{2,1,0:T(8,128)}), f32[16,24,128]{2,1,0:T(8,128)S(1)}, u32[]{:S(2)}, u32[]{:S(2)}) async-start(f32[16,24,128]{2,1,0:T(8,128)} %get-tuple-element.41), calls=%async_computation.1 | async-start | bytes 393216 | tf_op jit(solution)/shard_map/all_to_all | solution.py:627
  75.8 0.7 copy-start.6
  102.4 1.6 %collective-permute-start.3 = (f32[192,128]{1,0:T(8,128)}, f32[192,128]{1,0:T(8,128)S(1)}, u32[]{:S(2)}, u32[]{:S(2)}) collective-permute-start(f32[192,128]{1,0:T(8,128)} %shard_map.200), channel_id=1, source_target_pairs={{0,1},{1,0},{2,3},{3,2},{4,5},{5,4},{6,7},{7,6},{8,9},{9,8},{10,11... | collective-permute-start | bytes 294920 | tf_op jit(solution)/shard_map/ppermute | solution.py:379
  104.9 4.9 %collective-permute-start.4 = (f32[192,128]{1,0:T(8,128)S(1)}, f32[192,128]{1,0:T(8,128)S(1)}, u32[]{:S(2)}, u32[]{:S(2)}) collective-permute-start(f32[192,128]{1,0:T(8,128)S(1)} %add.26), channel_id=1, source_target_pairs={{0,2},{2,0},{4,6},{6,4},{8,10},{10,8},{12,14},{14,12},{16,18},{18,... | collective-permute-start | bytes 294920 | tf_op jit(solution)/shard_map/ppermute | solution.py:379
  109.8 4.7 %collective-permute-start.5 = (f32[192,128]{1,0:T(8,128)S(1)}, f32[192,128]{1,0:T(8,128)S(1)}, u32[]{:S(2)}, u32[]{:S(2)}) collective-permute-start(f32[192,128]{1,0:T(8,128)S(1)} %add.27), channel_id=1, source_target_pairs={{0,4},{2,6},{4,0},{6,2},{8,12},{10,14},{12,8},{14,10},{16,20},{18,... | collective-permute-start | bytes 294920 | tf_op jit(solution)/shard_map/ppermute | solution.py:379
  114.5 4.7 %collective-permute-start.6 = (f32[192,128]{1,0:T(8,128)S(1)}, f32[192,128]{1,0:T(8,128)S(1)}, u32[]{:S(2)}, u32[]{:S(2)}) collective-permute-start(f32[192,128]{1,0:T(8,128)S(1)} %add.28), channel_id=1, source_target_pairs={{0,8},{2,10},{4,12},{6,14},{8,0},{10,2},{12,4},{14,6},{16,24},{18,... | collective-permute-start | bytes 294920 | tf_op jit(solution)/shard_map/ppermute | solution.py:379
  119.2 6.6 %collective-permute-start.7 = (f32[192,128]{1,0:T(8,128)S(1)}, f32[192,128]{1,0:T(8,128)S(1)}, u32[]{:S(2)}, u32[]{:S(2)}) collective-permute-start(f32[192,128]{1,0:T(8,128)S(1)} %add.29), channel_id=1, source_target_pairs={{0,16},{2,18},{4,20},{6,22},{8,24},{10,26},{12,28},{14,30},{16,0},... | collective-permute-start | bytes 294920 | tf_op jit(solution)/shard_map/ppermute | solution.py:379

commit v2 on v1

--- a/solution.py
+++ b/solution.py
@@ -39,13 +39,15 @@
 
 
 def down(x):
-    rows = lax.broadcasted_iota(jnp.int32, x.shape, 0)
-    return jnp.where(rows == 0, 0.0, pltpu.roll(x, 1, 0))
+    turned = pltpu.roll(x, 1, 0)
+    rows = lax.broadcasted_iota(jnp.int32, (8, x.shape[1]), 0)
+    return jnp.concatenate([jnp.where(rows == 0, 0.0, turned[:8]), turned[8:]], axis=0)
 
 
 def up(x):
-    rows = lax.broadcasted_iota(jnp.int32, x.shape, 0)
-    return jnp.where(rows == x.shape[0] - 1, 0.0, pltpu.roll(x, x.shape[0] - 1, 0))
+    turned = pltpu.roll(x, x.shape[0] - 1, 0)
+    rows = lax.broadcasted_iota(jnp.int32, (8, x.shape[1]), 0)
+    return jnp.concatenate([turned[:-8], jnp.where(rows == 7, 0.0, turned[-8:])], axis=0)
 
 
 def lane_ids(count):
@@ -62,8 +64,8 @@
 
 def forward_kernel(height, own, channels, r_ref, low_ref, mid_ref, high_ref, first_ref, taps_ref, last_ref, b1_ref,
                    b2_ref, b3_ref, basis_ref, img_ref, col_ref, logdet_ref, wf_a, wf_b, wt_ref, wl_a, wl_b, *rest):
-    saved, scratch = rest[:-11], rest[-11:]
-    wm_ref, bf_ref, bm_ref, bl_ref, hm, h0, hp, h2s, wide_s, lat_s, mine_s = scratch
+    saved, scratch = rest[:-9], rest[-9:]
+    wm_ref, bf_ref, bm_ref, bl_ref, hs, h2s, wide_s, lat_s, mine_s = scratch
     step = pl.program_id(0)
     samples, cols = lat_s.shape[0], lat_s.shape[2]
     first = r_ref[0] * own
@@ -99,36 +101,36 @@
         if layer == 1:
             saved[10][0] = cond
         high, low = split(taps(cond))
-        both = jnp.concatenate([high, low], axis=1)
+        both = jnp.concatenate([high, low, high], axis=1)
         for k in range(plan["n1"]):
             if k % 2 == 0:
                 lanes = blk(k, min(2, plan["n1"] - k))
-                pair = dot(both, wf[: 2 * LANE, lanes]) + dot(high, wf[2 * LANE :, lanes])
+                pair = dot(both, wf[:, lanes])
             pre = pair[:, blk(k % 2)] + bf_ref[layer : layer + 1]
             sig = 0.5 + 0.5 * jnp.tanh(0.5 * pre)
-            mask = mask_of(plan["o1"], k)
-            hidden = pre * sig * mask
+            kept = sig * mask_of(plan["o1"], k)
+            hidden = pre * kept
             start, count = plan["s1"]
             if start <= k < start + count:
-                out_s1[0, :, blk(k - start)] = (sig * (1.0 + pre * (1.0 - sig)) * mask).astype(BF)
+                out_s1[0, :, blk(k - start)] = (kept + hidden * (1.0 - sig)).astype(BF)
             plain = hidden.astype(BF)
-            h0[:, blk(k)] = plain
-            hm[:, blk(k)] = down(hidden).astype(BF)
-            hp[:, blk(k)] = up(hidden).astype(BF)
+            hs[:, blk(3 * k)] = down(hidden).astype(BF)
+            hs[:, blk(3 * k + 1)] = plain
+            hs[:, blk(3 * k + 2)] = up(hidden).astype(BF)
             start, count = plan["h1"]
             if start <= k < start + count:
                 out_h1[0, :, blk(k - start)] = plain
         for k in range(plan["n2"]):
             wide = min(2, plan["n1"] - k)
-            pre = bm_ref[layer : layer + 1]
-            for tap, part in enumerate((hm, h0, hp)):
-                pre = pre + dot(part[:, blk(k, wide)], wm_ref[layer, tap, : wide * LANE])
+            pre = dot(hs[:, blk(3 * k, 3 * wide)], wm_ref[layer, : 3 * wide * LANE])
+            pre = pre + bm_ref[layer : layer + 1]
             sig = 0.5 + 0.5 * jnp.tanh(0.5 * pre)
-            mask = mask_of(plan["o2"], k)
-            hidden = (pre * sig * mask).astype(BF)
+            kept = sig * mask_of(plan["o2"], k)
+            hidden = pre * kept
             start, count = plan["s2"]
             if start <= k < start + count:
-                out_s2[0, :, blk(k - start)] = (sig * (1.0 + pre * (1.0 - sig)) * mask).astype(BF)
+                out_s2[0, :, blk(k - start)] = (kept + hidden * (1.0 - sig)).astype(BF)
+            hidden = hidden.astype(BF)
             h2s[:, blk(k)] = hidden
             start, count = plan["h2"]
             if start <= k < start + count:
@@ -168,7 +170,7 @@
 def backward_kernel(height, own, channels, reach, cells, r_ref, near_ref, loss_ref, wf_a, wf_b, wt_ref,
                     wl_a, wl_b, basis_ref, *rest):
     saved, lat_ref, out_ref, scratch = rest[:11], rest[11], rest[12], rest[13:]
-    near_s, cot_s, dm, d0, dp, cpo_s, acc_mid, acc_last, acc_first, acc_bias = scratch
+    near_s, cot_s, ds, cpo_s, acc_mid, acc_last, acc_first, acc_bias = scratch
     step = pl.program_id(0)
     first = r_ref[0] * own
     lane = lane_ids(LANE)
@@ -231,39 +233,50 @@
         acc_bias[layer, 2:3] += jnp.sum(mine, axis=0, keepdims=True)
         start2, count2 = plan["s2"]
         base1, _ = plan["h1"]
+        lefts, rights = [], []
         for k in range(start2, start2 + count2):
-            cot = dot(spread, wl[blk(k), :], NT) * s2[0, :, blk(k - start2)].astype(F32)
+            if (k - start2) % 2 == 0:
+                pair = dot(spread, wl[blk(k, 2), :], NT)
+            cot = pair[:, blk((k - start2) % 2)] * s2[0, :, blk(k - start2)].astype(F32)
             plain = cot.astype(BF)
             cot = plain.astype(F32)
             parts = (up(cot).astype(BF), plain, down(cot).astype(BF))
-            for ref, part in zip((dm, d0, dp), parts):
-                ref[:, blk(k - start2)] = part
+            for tap, part in enumerate(parts):
+                ds[:, blk(3 * (k - start2) + tap)] = part
             local = k - base1
             if 0 <= local < 4:
                 mask = own_of(plan["o2"], k)
                 acc_bias[layer, 1:2] += jnp.sum(cot * mask, axis=0, keepdims=True)
-                lhs = jnp.concatenate([part * mask.astype(BF) for part in parts], 1)
-                acc_mid[layer] += dot(lhs, h1[0, :, blk(local, 2)], TN)
+                lefts.append(jnp.concatenate([part * mask.astype(BF) for part in parts], 1))
+                rights.append(h1[0, :, blk(local, 2)])
+        acc_mid[layer] += dot(jnp.concatenate(lefts, axis=0), jnp.concatenate(rights, axis=0), TN)
         high, low = split(taps(cond))
+        own_cots = []
         start1, count1 = plan["s1"]
         for k in range(start1, start1 + count1):
-            back = min(1, k - start2)
-            cot = None
-            for tap, ref in enumerate((dm, d0, dp)):
-                term = dot(ref[:, blk(k - start2 - back, 1 + back)], wt_ref[layer, tap, (1 - back) * LANE :])
-                cot = term if cot is None else cot + term
+            side = (k - start1) % 2
+            if side == 0:
+                outs = min(2, start1 + count1 - k)
+                lowest, highest = max(k - 1, start2), k + outs - 1
+                window = ds[:, blk(3 * (lowest - start2), 3 * (highest - lowest + 1))]
+                band = wt_ref[layer, 3 * (lowest - k + 1) * LANE : 3 * (highest - k + 2) * LANE, : outs * LANE]
+                pair = dot(window, band)
+            cot = pair[:, blk(side)]
             plain = (cot * s1[0, :, blk(k - start1)].astype(F32)).astype(BF)
             cpo_s[:, blk(k - start1)] = plain
             if k - start1 < 4:
                 mask = own_of(plan["o1"], k)
                 mine = plain.astype(F32) * mask
                 acc_bias[layer, 0:1] += jnp.sum(mine, axis=0, keepdims=True)
-                mine = mine.astype(BF)
-                acc_first[layer, :, blk(k - start1)] += dot(high, mine, TN) + dot(low, mine, TN)
+                own_cots.append(mine.astype(BF))
+        own_cots = jnp.concatenate(own_cots, axis=1)
+        acc_first[layer] += dot(
+            jnp.concatenate([high, low], axis=0), jnp.concatenate([own_cots, own_cots], axis=0), TN)
         if layer == 1:
             full = cpo_s[:, blk(0, count1)]
             lanes = blk(start1, count1)
-            terms = dot(full, wf[:LANE, lanes], NT) + dot(full, wf[2 * LANE :, lanes], NT)
+            terms = dot(full, wf[LANE:, lanes], NT)
+            terms = terms[:, :LANE] + terms[:, LANE:]
             total = up(terms) + pltpu.roll(terms, LANE - SLOT, 1) * (lane < SLOT).astype(F32)
             total = jnp.where(lane < SLOT, total, 0.0)
             total = total + jnp.where(lane < SLOT, pltpu.roll(down(terms), LANE - 2 * SLOT, 1), 0.0)
@@ -358,10 +371,13 @@
                 band.append(total)
             top = jnp.concatenate(band[:GROUP], axis=0)
             low = jnp.concatenate(band[GROUP:], axis=0)
-            wm_ref[layer, dc, :LANE] = top.astype(BF)
-            wm_ref[layer, dc, LANE:] = low.astype(BF)
-            wt_ref[layer, dc, :LANE] = low.T.astype(BF)
-            wt_ref[layer, dc, LANE:] = top.T.astype(BF)
+            empty = jnp.zeros((LANE, LANE), BF)
+            wm_ref[layer, blk(dc)] = top.astype(BF)
+            wm_ref[layer, blk(3 + dc)] = low.astype(BF)
+            near, far = low.T.astype(BF), top.T.astype(BF)
+            for j, pair in enumerate(((near, empty), (far, near), (empty, far))):
+                wt_ref[layer, blk(3 * j + dc), :LANE] = pair[0]
+                wt_ref[layer, blk(3 * j + dc), LANE:] = pair[1]
         columns = [dot(last_ref[layer, dr], parts, TN) for dr in range(3)]
         for row in range(plan["n2"] * GROUP):
             total = jnp.zeros((channels, 3 * LANE), F32)
@@ -375,6 +391,10 @@
     for axis in axes:
         count = lax.axis_size(axis)
         hop = 1
+        if count % 4 == 0:
+            near = [lax.ppermute(value, axis, [(i, i ^ far) for i in range(count)]) for far in (1, 2, 3)]
+            value = (value + near[0]) + (near[1] + near[2])
+            hop = 4
         while hop < count:
             value = value + lax.ppermute(value, axis, [(i, i ^ hop) for i in range(count)])
             hop *= 2
@@ -384,10 +404,9 @@
 def grid_kernel(n_freq, pad_freq, height, img_width, r_ref, u_ref, v_ref, obs_ref, w_ref, out_ref, const_ref,
                 u_s, c_s, sign_s):
     share = u_s.shape[0]
-    start = pl.multiple_of(r_ref[1] * share, share)
     half = img_width // 2
-    u = u_ref[pl.ds(start, share), :]
-    v = v_ref[pl.ds(start, share), :]
+    u = u_ref[...]
+    v = v_ref[...]
     mirror = v > half
     v_fold = jnp.where(mirror, img_width - v, v)
     col = v_fold - r_ref[0] * n_freq
@@ -410,8 +429,8 @@
             hots.append(jnp.concatenate(
                 [jnp.where(ids + jnp.int16(16 * g) == u_row, one, zero) for g in range(height // 16)], axis=0))
             c_hot = slots == c_s[row, :]
-            lanes = pl.ds(pl.multiple_of((start + j * group + q) * LANE, LANE), LANE)
-            w = w_ref[pl.ds(start + j * group + q, 1), :]
+            lanes = pl.ds(pl.multiple_of((j * group + q) * LANE, LANE), LANE)
+            w = w_ref[row, :]
             o_re, o_im = obs_ref[0:1, lanes], obs_ref[1:2, lanes]
             total = total + w * (o_re * o_re + o_im * o_im)
             parts = []
@@ -452,17 +471,22 @@
     pad_freq = slot_count(n_freq)
     rows = vis_u.shape[0] // LANE
     share = rows // n_grp
-    vmem = pl.BlockSpec(memory_space=pltpu.VMEM)
+    rows_spec = pl.BlockSpec((share, LANE), lambda i, r: (r[1], 0))
     where = jnp.stack([lax.axis_index("rows"), lax.axis_index("grp")]).astype(jnp.int32)
     return pl.pallas_call(
         functools.partial(grid_kernel, n_freq, pad_freq, height, img_width),
         out_shape=(jax.ShapeDtypeStruct((height, 6 * pad_freq), F32),
                    jax.ShapeDtypeStruct((1, 1), F32)),
-        in_specs=[pl.BlockSpec(memory_space=pltpu.SMEM)] + [vmem] * 4,
-        out_specs=(vmem, vmem),
-        scratch_shapes=[pltpu.VMEM((share, LANE), jnp.int32), pltpu.VMEM((share, LANE), jnp.int32),
-                        pltpu.VMEM((share, LANE), F32)],
-        compiler_params=pltpu.CompilerParams(vmem_limit_bytes=24 * 2**20),
+        grid_spec=pltpu.PrefetchScalarGridSpec(
+            num_scalar_prefetch=1,
+            grid=(1,),
+            in_specs=[rows_spec, rows_spec, pl.BlockSpec((2, share * LANE), lambda i, r: (0, r[1])), rows_spec],
+            out_specs=(pl.BlockSpec((height, 6 * pad_freq), lambda i, r: (0, 0)),
+                       pl.BlockSpec((1, 1), lambda i, r: (0, 0))),
+            scratch_shapes=[pltpu.VMEM((share, LANE), jnp.int32), pltpu.VMEM((share, LANE), jnp.int32),
+                            pltpu.VMEM((share, LANE), F32)],
+        ),
+        compiler_params=pltpu.CompilerParams(vmem_limit_bytes=60 * 2**20),
         cost_estimate=pl.CostEstimate(flops=2 * height * 256 * share * LANE * 4,
                                       bytes_accessed=24 * share * LANE, transcendentals=0),
     )(where, vis_u.reshape(rows, LANE), vis_v.reshape(rows, LANE), observed, vis_weight.reshape(rows, LANE))
@@ -580,7 +604,7 @@
     saved_types = [jax.ShapeDtypeStruct((samples,) + shape, kind) for shape, kind in saved_shapes]
     weights = weights + (basis,)
     bands = [((3 * LANE, plan["n1"] * LANE), BF) for plan in PLAN]
-    bands += [((layers, 3, 2 * LANE, LANE), BF)]
+    bands += [((layers, 9 * LANE, 2 * LANE), BF)]
     bands += [((plan["n2"] * LANE, 3 * LANE), BF) for plan in PLAN]
     bands = [jax.ShapeDtypeStruct(shape, kind) for shape, kind in bands]
     max1 = max(plan["n1"] for plan in PLAN) * LANE
@@ -604,9 +628,9 @@
             *[whole(band) for band in bands],
             *saved_specs,
         ),
-        scratch_shapes=[pltpu.VMEM((layers, 3, 2 * LANE, LANE), BF)]
+        scratch_shapes=[pltpu.VMEM((layers, 6 * LANE, LANE), BF)]
         + [pltpu.VMEM((layers, LANE), F32)] * 3
-        + [pltpu.VMEM((half, max1), BF)] * 3
+        + [pltpu.VMEM((half, 3 * max1), BF)]
         + [
             pltpu.VMEM((half, max2), BF),
             pltpu.VMEM((LANE, img_width), F32),
@@ -642,7 +666,7 @@
         scratch_shapes=[
             pltpu.VMEM((LANE, img_width), F32),
             pltpu.VMEM((img_width, LANE), F32),
-            *[pltpu.VMEM((half, max2), BF)] * 3,
+            pltpu.VMEM((half, 3 * max2), BF),
             pltpu.VMEM((half, max1), BF),
             pltpu.VMEM((layers, 3 * LANE, 2 * LANE), F32),
             pltpu.VMEM((layers, 3 * LANE, 4 * LANE), F32),

time: 130 us -> 120 us (0.923)
  Pallas kernels: 61.6 us -> 56.4 us
  local copies, waits for them, and re-layouts: 10.5 us -> 6.59 us
  waiting for transfers between devices: 31.1 us -> 28.5 us
    ppermute x6 -> x4, waiting for transfers between devices: 19.6 us -> 12.7 us  [butterfly(): lax.ppermute(value, axis, [(i, i ^ hop) for i in range(count)])]
    pallas_call x1, Pallas kernels: 25.9 us -> 20.5 us  [body(): pl.pallas_call(functools.partial(backward_kernel, height, row_count, chan...]
    ppermute x0 -> x3, waiting for transfers between devices: none -> 4.25 us  [butterfly(): lax.ppermute(value, axis, [(i, i ^ far) for i in range(count)])]
    unnamed x30 -> x24, local copies, waits for them, and re-layouts: 6.51 us -> 2.61 us
    ppermute x0 -> x3, starting transfers between devices: none -> 3.55 us  [butterfly(): lax.ppermute(value, axis, [(i, i ^ far) for i in range(count)])]
    ppermute x6 -> x4, starting transfers between devices: 4.42 us -> 1.66 us  [butterfly(): lax.ppermute(value, axis, [(i, i ^ hop) for i in range(count)])]
    pallas_call x1, Pallas kernels: 7.29 us -> 8.86 us  [gridded(): pl.pallas_call(functools.partial(grid_kernel, n_freq, pad_freq, height, i...]
  transfers between devices with their start and end apart: 10 -> 11, of which waited for: 8 -> 8; matrix products, arithmetic and copies ran while one was open for 1% -> 2% of each run, Pallas kernels for 6% -> 7%
where the time goes in v2:
time: 120 us
  Pallas kernels  56.4 us (47%)
  waiting for transfers between devices  28.5 us (24%)
  starting transfers between devices  23.1 us (19%)
  local copies, waits for them, and re-layouts  6.59 us (5%)
  between operations  2.79 us (2%)
  other arithmetic  2.17 us (2%)
    pallas_call x1, Pallas kernels, body(): pl.pallas_call(functools.partial(forward_kernel, height, row_count, chann...  24.4 us
    pallas_call x1, Pallas kernels, body(): pl.pallas_call(functools.partial(backward_kernel, height, row_count, chan...  20.5 us
    ppermute x4, waiting for transfers between devices, butterfly(): lax.ppermute(value, axis, [(i, i ^ hop) for i in range(count)])  12.7 us
    pallas_call x1, Pallas kernels, gridded(): pl.pallas_call(functools.partial(grid_kernel, n_freq, pad_freq, height, i...  8.86 us
    all_to_all x1, starting transfers between devices, body(): columns = lax.all_to_all(columns, 'rows', 0, 0, tiled=True)  8.02 us
    all_to_all x1, waiting for transfers between devices, body(): columns = lax.all_to_all(columns, 'rows', 0, 0, tiled=True)  6.23 us
    all_to_all x1, waiting for transfers between devices, body(): near = lax.all_to_all(near, 'rows', 0, 0, tiled=True)  5.3 us
    ppermute x1, starting transfers between devices, body(): low = lax.ppermute(latent, 'rows', forward)  4.85 us
  transfers between devices with their start and end apart: 11, of which 8 were waited for; matrix products, arithmetic and copies ran while one was open for 2% of the time, Pallas kernels for 7%

profile of v2, /device:TPU:0, one launch (start us, length us, event | category | flops | bytes accessed | tf_op | source)
XLA Modules:
  0.0 119.6 jit_solution(7801399831054194023)
XLA Ops:
  0.6 4.8 %collective-permute-start = (f32[4,12,512]{2,0,1:T(4,128)}, f32[4,12,512]{2,0,1:T(4,128)S(1)}, u32[]{:S(2)}, u32[]{:S(2)}) collective-permute-start(f32[4,12,512]{2,0,1:T(4,128)} %param.14), channel_id=1, source_target_pairs={{0,2},{2,4},{4,6},{6,8},{8,10},{10,12},{12,14},{14,16},{16,18},{18... | collective-permute-start | bytes 294920 | tf_op jit(solution)/shard_map/ppermute | solution.py:571
  5.5 1.3 %collective-permute-start.1 = (f32[4,12,512]{2,0,1:T(4,128)}, f32[4,12,512]{2,0,1:T(4,128)S(1)}, u32[]{:S(2)}, u32[]{:S(2)}) collective-permute-start(f32[4,12,512]{2,0,1:T(4,128)} %param.14), channel_id=1, source_target_pairs={{2,0},{4,2},{6,4},{8,6},{10,8},{12,10},{14,12},{16,14},{18,16},{20... | collective-permute-start | bytes 294920 | tf_op jit(solution)/shard_map/ppermute | solution.py:572
  6.8 0.6 pad_add_fusion.r_ref
  7.4 8.9 %shard_map.197 = (f32[192,144]{1,0:T(8,128)}, f32[1,1]{1,0:T(1,128)}) custom-call(s32[2]{0:T(128)} %pad_add_fusion.r_ref, s32[512,128]{1,0:T(8,128)} %bitcast.49, s32[512,128]{1,0:T(8,128)} %bitcast.50, f32[2,65536]{1,0:T(2,128)} %obs_ref.1, f32[512,128]{1,0:T(8,128)} %bitcast.51), custom_call_target="tpu_custom_call" | custom-call | flops 12884901888 | bytes 786432 | tf_op jit(solution)/shard_map/pallas_call | solution.py:476
  16.3 0.6 copy.40.first_ref
  16.9 0.6 pad.4.last_ref
  17.5 0.6 copy-done.4
  18.2 24.4 %shard_map.198 = (f32[12,4,512]{2,1,0:T(4,128)}, f32[16,12,128]{2,1,0:T(8,128)}, f32[1,128]{1,0:T(1,128)}, bf16[384,1024]{1,0:T(8,128)(2,1)}, bf16[384,896]{1,0:...) custom-call(s32[1]{0:T(128)} %bitcast.r_ref, ...), custom_call_target="tpu_custom_call" | custom-call | tf_op jit(solution)/shard_map/pallas_call | solution.py:613
  42.6 8.0 %all-to-all-start = ((f32[16,12,128]{2,1,0:T(8,128)}), f32[16,12,128]{2,1,0:T(8,128)S(1)}, u32[]{:S(2)}, u32[]{:S(2)}) async-start(f32[16,12,128]{2,1,0:T(8,128)} %get-tuple-element.39), calls=%async_computation | async-start | bytes 262144 | tf_op jit(solution)/shard_map/all_to_all | solution.py:647
  50.8 1.4 %collective-permute-done.2 = f32[192,144]{1,0:T(8,128)S(1)} collective-permute-done((f32[192,144]{1,0:T(8,128)S(1)}, f32[192,144]{1,0:T(8,128)S(1)}, u32[]{:S(2)}, u32[]{:S(2)}) %collective-permute-start.2) | collective-permute-done | bytes 110624 | tf_op jit(solution)/shard_map/ppermute | solution.py:399
  52.2 6.2 %all-to-all-done = f32[16,12,128]{2,1,0:T(8,128)S(1)} async-done(((f32[16,12,128]{2,1,0:T(8,128)}), f32[16,12,128]{2,1,0:T(8,128)S(1)}, u32[]{:S(2)}, u32[]{:S(2)}) %all-to-all-start) | async-done | bytes 98336 | tf_op jit(solution)/shard_map/all_to_all | solution.py:647
  58.5 2.7 %shard_map.199 = (f32[16,24,128]{2,1,0:T(8,128)}, f32[1,1]{1,0:T(1,128)}) custom-call(s32[1]{0:T(128)} %bitcast.r_ref, f32[192,128]{1,0:T(8,128)S(1)} %reshape.62.z_ref, f32[4,192,192]{2,1,0:T(8,128)S(1)} %copy-done, f32[192,144]{1,0:T(8,128)S(1)} %add.27.grid_ref, f32[2,3,144,128]{3,2,1,0:T(8,128)S(1)} %copy-done.1), custom_call_target="tpu_custom_call" | custom-call | tf_op jit(solution)/shard_map/pallas_call | solution.py:542
  61.2 3.7 %all-to-all-start.1 = ((f32[16,24,128]{2,1,0:T(8,128)}), f32[16,24,128]{2,1,0:T(8,128)S(1)}, u32[]{:S(2)}, u32[]{:S(2)}) async-start(f32[16,24,128]{2,1,0:T(8,128)} %get-tuple-element.41), calls=%async_computation.1 | async-start | bytes 393216 | tf_op jit(solution)/shard_map/all_to_all | solution.py:651
  65.5 0.6 reduce_sum.9
  67.4 5.3 %all-to-all-done.1.near_ref = f32[16,24,128]{2,1,0:T(8,128)S(1)} async-done(((f32[16,24,128]{2,1,0:T(8,128)}), f32[16,24,128]{2,1,0:T(8,128)S(1)}, u32[]{:S(2)}, u32[]{:S(2)}) %all-to-all-start.1) | async-done | bytes 196640 | tf_op jit(solution)/shard_map/all_to_all | solution.py:651
  72.7 0.7 copy-done.2
  73.4 20.5 %shard_map.200 = f32[192,128]{1,0:T(8,128)} custom-call(s32[1]{0:T(128)} %bitcast.r_ref, f32[16,24,128]{2,1,0:T(8,128)} %copy-done.2, f32[1,1]{1,0:T(1,128)} %bitcast.12.loss_ref, bf16[384,1024]{1,0:T(8,128)(2,1)} %get-tuple-element.45.wf_a, bf16[384,896]{1,0:T(8,128)(2,1)} %get-tuple-element.46.wf_b, bf16[2,1152,256]{2,1,0:T(8,128)(2,1)} %get-tuple-element.47.wt_ref, ...), custom_call_target="tpu_custom_call" | custom-call | tf_op jit(solution)/shard_map/pallas_call | solution.py:657
  94.0 1.5 %collective-permute-done.3 = f32[192,128]{1,0:T(8,128)S(1)} collective-permute-done((f32[192,128]{1,0:T(8,128)}, f32[192,128]{1,0:T(8,128)S(1)}, u32[]{:S(2)}, u32[]{:S(2)}) %collective-permute-start.3) | collective-permute-done | bytes 98336 | tf_op jit(solution)/shard_map/ppermute | solution.py:399
  95.5 0.9 add.29
  96.4 0.9 collective-permute-start.6
  97.2 2.0 %collective-permute-start.5 = (f32[192,128]{1,0:T(8,128)S(1)}, f32[192,128]{1,0:T(8,128)S(1)}, u32[]{:S(2)}, u32[]{:S(2)}) collective-permute-start(f32[192,128]{1,0:T(8,128)S(1)} %add.29), channel_id=1, source_target_pairs={{0,4},{2,6},{4,0},{6,2},{8,12},{10,14},{12,8},{14,10},{16,20},{18,... | collective-permute-start | bytes 294920 | tf_op jit(solution)/shard_map/ppermute | solution.py:395
  99.2 0.7 collective-permute-start.4
  99.9 3.1 %collective-permute-done.6 = f32[192,128]{1,0:T(8,128)S(1)} collective-permute-done((f32[192,128]{1,0:T(8,128)S(1)}, f32[192,128]{1,0:T(8,128)S(1)}, u32[]{:S(2)}, u32[]{:S(2)}) %collective-permute-start.6) | collective-permute-done | bytes 98336 | tf_op jit(solution)/shard_map/ppermute | solution.py:395
  103.0 1.2 collective-permute-done.5
  104.2 0.6 collective-permute-start.7
  104.8 4.1 %collective-permute-done.7 = f32[192,128]{1,0:T(8,128)S(1)} collective-permute-done((f32[192,128]{1,0:T(8,128)S(1)}, f32[192,128]{1,0:T(8,128)S(1)}, u32[]{:S(2)}, u32[]{:S(2)}) %collective-permute-start.7) | collective-permute-done | bytes 98336 | tf_op jit(solution)/shard_map/ppermute | solution.py:399
  108.9 0.9 collective-permute-start.8
  109.8 5.7 %collective-permute-done.8 = f32[192,128]{1,0:T(8,128)S(1)} collective-permute-done((f32[192,128]{1,0:T(8,128)S(1)}, f32[192,128]{1,0:T(8,128)S(1)}, u32[]{:S(2)}, u32[]{:S(2)}) %collective-permute-start.8) | collective-permute-done | bytes 98336 | tf_op jit(solution)/shard_map/ppermute | solution.py:399
  115.6 0.6 slice.33
  117.4 0.6 copy.47
  118.0 0.6 copy.48
  118.8 0.7 copy.42
  (37 shorter events, 1.7 us)
Async XLA Ops:
  0.6 16.9 %collective-permute-start = (f32[4,12,512]{2,0,1:T(4,128)}, f32[4,12,512]{2,0,1:T(4,128)S(1)}, u32[]{:S(2)}, u32[]{:S(2)}) collective-permute-start(f32[4,12,512]{2,0,1:T(4,128)} %param.14), channel_id=1, source_target_pairs={{0,2},{2,4},{4,6},{6,8},{8,10},{10,12},{12,14},{14,16},{16,18},{18... | collective-permute-start | bytes 294920 | tf_op jit(solution)/shard_map/ppermute | solution.py:571
  5.5 12.0 %collective-permute-start.1 = (f32[4,12,512]{2,0,1:T(4,128)}, f32[4,12,512]{2,0,1:T(4,128)S(1)}, u32[]{:S(2)}, u32[]{:S(2)}) collective-permute-start(f32[4,12,512]{2,0,1:T(4,128)} %param.14), channel_id=1, source_target_pairs={{2,0},{4,2},{6,4},{8,6},{10,8},{12,10},{14,12},{16,14},{18,16},{20... | collective-permute-start | bytes 294920 | tf_op jit(solution)/shard_map/ppermute | solution.py:572
  7.4 8.9 %copy-start.6 = (f32[2,9,32,1]{2,3,1,0:T(1,128)S(1)}, f32[2,9,32,1]{2,3,1,0:T(1,128)}, u32[]{:S(2)}) copy-start(f32[2,9,32,1]{2,3,1,0:T(1,128)} %param.15) | copy-start | bytes 6916
  7.4 9.5 %copy-start.7 = (bf16[2,9,2,32]{3,2,1,0:T(2,128)(2,1)S(1)}, bf16[2,9,2,32]{3,2,1,0:T(2,128)(2,1)}, u32[]{:S(2)}) copy-start(bf16[2,9,2,32]{3,2,1,0:T(2,128)(2,1)} %param.19) | copy-start | bytes 6916
  16.2 34.4 %copy-start.3 = (f32[192,144]{1,0:T(8,128)S(1)}, f32[192,144]{1,0:T(8,128)}, u32[]{:S(2)}) copy-start(f32[192,144]{1,0:T(8,128)} %get-tuple-element.40) | copy-start | bytes 331780
  17.5 41.0 %copy-start = (f32[4,192,192]{2,1,0:T(8,128)S(1)}, f32[4,192,192]{2,1,0:T(8,128)}, u32[]{:S(2)}) copy-start(f32[4,192,192]{2,1,0:T(8,128)} %constant.35.clone.cs_ref) | copy-start | bytes 1769476
  17.5 41.0 %copy-start.1 = (f32[2,3,144,128]{3,2,1,0:T(8,128)S(1)}, f32[2,3,144,128]{3,2,1,0:T(8,128)}, u32[]{:S(2)}) copy-start(f32[2,3,144,128]{3,2,1,0:T(8,128)} %constant.36.clone.sel_ref) | copy-start | bytes 1327108
  17.5 0.6 copy-start.4
  17.5 0.7 copy-start.5
  42.6 15.8 %all-to-all-start = ((f32[16,12,128]{2,1,0:T(8,128)}), f32[16,12,128]{2,1,0:T(8,128)S(1)}, u32[]{:S(2)}, u32[]{:S(2)}) async-start(f32[16,12,128]{2,1,0:T(8,128)} %get-tuple-element.39), calls=%async_computation | async-start | bytes 262144 | tf_op jit(solution)/shard_map/all_to_all | solution.py:647
  50.7 14.8 %copy-start.8 = (f32[1,128]{1,0:T(1,128)S(1)}, f32[1,128]{1,0:T(1,128)}, u32[]{:S(2)}) copy-start(f32[1,128]{1,0:T(1,128)} %get-tuple-element.44) | copy-start | bytes 1540
  50.7 1.5 %collective-permute-start.2 = (f32[192,144]{1,0:T(8,128)S(1)}, f32[192,144]{1,0:T(8,128)S(1)}, u32[]{:S(2)}, u32[]{:S(2)}) collective-permute-start(f32[192,144]{1,0:T(8,128)S(1)} %copy-done.3), channel_id=1, source_target_pairs={{0,1},{1,0},{2,3},{3,2},{4,5},{5,4},{6,7},{7,6},{8,9},{9,8},{10,11... | collective-permute-start | bytes 331784 | tf_op jit(solution)/shard_map/ppermute | solution.py:399
  61.2 11.6 %all-to-all-start.1 = ((f32[16,24,128]{2,1,0:T(8,128)}), f32[16,24,128]{2,1,0:T(8,128)S(1)}, u32[]{:S(2)}, u32[]{:S(2)}) async-start(f32[16,24,128]{2,1,0:T(8,128)} %get-tuple-element.41), calls=%async_computation.1 | async-start | bytes 393216 | tf_op jit(solution)/shard_map/all_to_all | solution.py:651
  72.7 0.7 copy-start.2
  93.9 1.6 %collective-permute-start.3 = (f32[192,128]{1,0:T(8,128)}, f32[192,128]{1,0:T(8,128)S(1)}, u32[]{:S(2)}, u32[]{:S(2)}) collective-permute-start(f32[192,128]{1,0:T(8,128)} %shard_map.200), channel_id=1, source_target_pairs={{0,1},{1,0},{2,3},{3,2},{4,5},{5,4},{6,7},{7,6},{8,9},{9,8},{10,11... | collective-permute-start | bytes 294920 | tf_op jit(solution)/shard_map/ppermute | solution.py:399
  96.4 6.6 %collective-permute-start.6 = (f32[192,128]{1,0:T(8,128)S(1)}, f32[192,128]{1,0:T(8,128)S(1)}, u32[]{:S(2)}, u32[]{:S(2)}) collective-permute-start(f32[192,128]{1,0:T(8,128)S(1)} %add.29), channel_id=1, source_target_pairs={{0,6},{2,4},{4,2},{6,0},{8,14},{10,12},{12,10},{14,8},{16,22},{18,... | collective-permute-start | bytes 294920 | tf_op jit(solution)/shard_map/ppermute | solution.py:395
  97.2 6.9 %collective-permute-start.5 = (f32[192,128]{1,0:T(8,128)S(1)}, f32[192,128]{1,0:T(8,128)S(1)}, u32[]{:S(2)}, u32[]{:S(2)}) collective-permute-start(f32[192,128]{1,0:T(8,128)S(1)} %add.29), channel_id=1, source_target_pairs={{0,4},{2,6},{4,0},{6,2},{8,12},{10,14},{12,8},{14,10},{16,20},{18,... | collective-permute-start | bytes 294920 | tf_op jit(solution)/shard_map/ppermute | solution.py:395
  99.2 4.9 %collective-permute-start.4 = (f32[192,128]{1,0:T(8,128)S(1)}, f32[192,128]{1,0:T(8,128)S(1)}, u32[]{:S(2)}, u32[]{:S(2)}) collective-permute-start(f32[192,128]{1,0:T(8,128)S(1)} %add.29), channel_id=1, source_target_pairs={{0,2},{2,0},{4,6},{6,4},{8,10},{10,8},{12,14},{14,12},{16,18},{18,... | collective-permute-start | bytes 294920 | tf_op jit(solution)/shard_map/ppermute | solution.py:395
  104.2 4.7 %collective-permute-start.7 = (f32[192,128]{1,0:T(8,128)S(1)}, f32[192,128]{1,0:T(8,128)S(1)}, u32[]{:S(2)}, u32[]{:S(2)}) collective-permute-start(f32[192,128]{1,0:T(8,128)S(1)} %add_add_fusion), channel_id=1, source_target_pairs={{0,8},{2,10},{4,12},{6,14},{8,0},{10,2},{12,4},{14,6},{16,24},{18,... | collective-permute-start | bytes 294920 | tf_op jit(solution)/shard_map/ppermute | solution.py:399
  108.9 6.6 %collective-permute-start.8 = (f32[192,128]{1,0:T(8,128)S(1)}, f32[192,128]{1,0:T(8,128)S(1)}, u32[]{:S(2)}, u32[]{:S(2)}) collective-permute-start(f32[192,128]{1,0:T(8,128)S(1)} %add.33), channel_id=1, source_target_pairs={{0,16},{2,18},{4,20},{6,22},{8,24},{10,26},{12,28},{14,30},{16,0},... | collective-permute-start | bytes 294920 | tf_op jit(solution)/shard_map/ppermute | solution.py:399

commit v3 on v2

--- a/solution.py
+++ b/solution.py
@@ -345,7 +345,7 @@
     edge = lax.broadcasted_iota(jnp.int32, (SLOT, LANE), 0)
     for layer, (wf, wl) in enumerate(((wf_a, wl_a), (wf_b, wl_b))):
         plan = PLAN[layer]
-        rows = tiled(first_ref[layer])
+        rows = [tiled(first_ref[layer, tap]) for tap in range(9)]
         for k in range(plan["n1"]):
             row = k * GROUP + lane // channels + plan["o1"] + own - 1
             pieces = []
@@ -353,7 +353,7 @@
                 total = jnp.zeros((SLOT, LANE), F32)
                 for dr in range(3):
                     hit = (edge == row + dr) & (edge < 3 * own)
-                    total = total + jnp.where(hit, rows[3 * dr + dc : 3 * dr + dc + 1], 0.0)
+                    total = total + jnp.where(hit, rows[3 * dr + dc], 0.0)
                 pieces.append(total)
             pieces.append(jnp.zeros((LANE - 3 * SLOT, LANE), F32))
             high, low = split(jnp.concatenate(pieces, axis=0))
@@ -378,7 +378,11 @@
             for j, pair in enumerate(((near, empty), (far, near), (empty, far))):
                 wt_ref[layer, blk(3 * j + dc), :LANE] = pair[0]
                 wt_ref[layer, blk(3 * j + dc), LANE:] = pair[1]
-        columns = [dot(last_ref[layer, dr], parts, TN) for dr in range(3)]
+        blank = jnp.zeros((2, channels), F32)
+        columns = []
+        for dr in range(3):
+            pieces = [last_ref[layer, 3 * dr + dc].astype(F32) for dc in range(3)] + [blank]
+            columns.append(dot(jnp.concatenate(pieces, axis=0).astype(BF), parts, TN))
         for row in range(plan["n2"] * GROUP):
             total = jnp.zeros((channels, 3 * LANE), F32)
             for dr in range(3):
@@ -576,8 +580,7 @@
     low, high, grid = lax.optimization_barrier((low, high, grid))
     grid = butterfly(grid, ("grp",))
     pieces = [value.transpose(1, 0, 2) for value in (low, latent, high)]
-    last = jnp.pad(w_last.reshape(layers, 3, 6, channels), ((0, 0), (0, 0), (0, 2), (0, 0)))
-    weights = (w_first.reshape(layers, 9, channels), w_mid, last, b_first, b_mid, b_last)
+    weights = (w_first.reshape(layers, 9, 1, channels), w_mid, w_last, b_first, b_mid, b_last)
     basis_np = column_basis(img_width)
     basis_high = basis_np.astype(BF)
     basis_low = (basis_np - basis_high.astype(np.float32)).astype(BF)

time: 120 us -> 119 us (level)
  local copies, waits for them, and re-layouts: 6.59 us -> 5.34 us
    unnamed x24 -> x18, local copies, waits for them, and re-layouts: 2.61 us -> 2.58 us
  transfers between devices with their start and end apart: 11 -> 11, of which waited for: 8 -> 8; matrix products, arithmetic and copies ran while one was open for 2% -> 1% of each run, Pallas kernels for 7% -> 7%
where the time goes in v3:
time: 119 us; the launch traced here: 118 us
  Pallas kernels  56.5 us (47%)
  waiting for transfers between devices  28.5 us (24%)
  starting transfers between devices  23.1 us (19%)
  local copies, waits for them, and re-layouts  5.34 us (4%)
  between operations  2.79 us (2%)
  other arithmetic  2.17 us (2%)
    pallas_call x1, Pallas kernels, body(): pl.pallas_call(functools.partial(forward_kernel, height, row_count, chann...  24.7 us
    pallas_call x1, Pallas kernels, body(): pl.pallas_call(functools.partial(backward_kernel, height, row_count, chan...  20.5 us
    ppermute x4, waiting for transfers between devices, butterfly(): lax.ppermute(value, axis, [(i, i ^ hop) for i in range(count)])  12.7 us
    pallas_call x1, Pallas kernels, gridded(): pl.pallas_call(functools.partial(grid_kernel, n_freq, pad_freq, height, i...  8.73 us
    all_to_all x1, starting transfers between devices, body(): columns = lax.all_to_all(columns, 'rows', 0, 0, tiled=True)  8.03 us
    all_to_all x1, waiting for transfers between devices, body(): columns = lax.all_to_all(columns, 'rows', 0, 0, tiled=True)  6.23 us
    all_to_all x1, waiting for transfers between devices, body(): near = lax.all_to_all(near, 'rows', 0, 0, tiled=True)  5.3 us
    ppermute x1, starting transfers between devices, body(): low = lax.ppermute(latent, 'rows', forward)  4.85 us
  transfers between devices with their start and end apart: 11, of which 8 were waited for; matrix products, arithmetic and copies ran while one was open for 1% of the time, Pallas kernels for 7%

profile of v3, /device:TPU:0, one launch (start us, length us, event | category | flops | bytes accessed | tf_op | source)
XLA Modules:
  0.0 118.4 jit_solution(10119446454925270231)
XLA Ops:
  0.6 4.8 %collective-permute-start = (f32[4,12,512]{2,0,1:T(4,128)}, f32[4,12,512]{2,0,1:T(4,128)S(1)}, u32[]{:S(2)}, u32[]{:S(2)}) collective-permute-start(f32[4,12,512]{2,0,1:T(4,128)} %param.14), channel_id=1, source_target_pairs={{0,2},{2,4},{4,6},{6,8},{8,10},{10,12},{12,14},{14,16},{16,18},{18... | collective-permute-start | bytes 294920 | tf_op jit(solution)/shard_map/ppermute | solution.py:575
  5.5 1.3 %collective-permute-start.1 = (f32[4,12,512]{2,0,1:T(4,128)}, f32[4,12,512]{2,0,1:T(4,128)S(1)}, u32[]{:S(2)}, u32[]{:S(2)}) collective-permute-start(f32[4,12,512]{2,0,1:T(4,128)} %param.14), channel_id=1, source_target_pairs={{2,0},{4,2},{6,4},{8,6},{10,8},{12,10},{14,12},{16,14},{18,16},{20... | collective-permute-start | bytes 294920 | tf_op jit(solution)/shard_map/ppermute | solution.py:576
  6.8 0.6 pad_add_fusion.r_ref
  7.4 8.7 %shard_map.197 = (f32[192,144]{1,0:T(8,128)}, f32[1,1]{1,0:T(1,128)}) custom-call(s32[2]{0:T(128)} %pad_add_fusion.r_ref, s32[512,128]{1,0:T(8,128)} %bitcast.45, s32[512,128]{1,0:T(8,128)} %bitcast.46, f32[2,65536]{1,0:T(2,128)} %obs_ref.1, f32[512,128]{1,0:T(8,128)} %bitcast.47), custom_call_target="tpu_custom_call" | custom-call | flops 12884901888 | bytes 786432 | tf_op jit(solution)/shard_map/pallas_call | solution.py:480
  16.2 0.6 copy-done.4
  16.8 24.7 %shard_map.198 = (f32[12,4,512]{2,1,0:T(4,128)}, f32[16,12,128]{2,1,0:T(8,128)}, f32[1,128]{1,0:T(1,128)}, bf16[384,1024]{1,0:T(8,128)(2,1)}, bf16[384,896]{1,0:...) custom-call(s32[1]{0:T(128)} %bitcast.r_ref, ...), custom_call_target="tpu_custom_call" | custom-call | tf_op jit(solution)/shard_map/pallas_call | solution.py:616
  41.5 8.0 %all-to-all-start = ((f32[16,12,128]{2,1,0:T(8,128)}), f32[16,12,128]{2,1,0:T(8,128)S(1)}, u32[]{:S(2)}, u32[]{:S(2)}) async-start(f32[16,12,128]{2,1,0:T(8,128)} %get-tuple-element.39), calls=%async_computation | async-start | bytes 262144 | tf_op jit(solution)/shard_map/all_to_all | solution.py:650
  49.6 1.4 %collective-permute-done.2 = f32[192,144]{1,0:T(8,128)S(1)} collective-permute-done((f32[192,144]{1,0:T(8,128)S(1)}, f32[192,144]{1,0:T(8,128)S(1)}, u32[]{:S(2)}, u32[]{:S(2)}) %collective-permute-start.2) | collective-permute-done | bytes 110624 | tf_op jit(solution)/shard_map/ppermute | solution.py:403
  51.1 6.2 %all-to-all-done = f32[16,12,128]{2,1,0:T(8,128)S(1)} async-done(((f32[16,12,128]{2,1,0:T(8,128)}), f32[16,12,128]{2,1,0:T(8,128)S(1)}, u32[]{:S(2)}, u32[]{:S(2)}) %all-to-all-start) | async-done | bytes 98336 | tf_op jit(solution)/shard_map/all_to_all | solution.py:650
  57.3 2.7 %shard_map.199 = (f32[16,24,128]{2,1,0:T(8,128)}, f32[1,1]{1,0:T(1,128)}) custom-call(s32[1]{0:T(128)} %bitcast.r_ref, f32[192,128]{1,0:T(8,128)S(1)} %reshape.58.z_ref, f32[4,192,192]{2,1,0:T(8,128)S(1)} %copy-done, f32[192,144]{1,0:T(8,128)S(1)} %add.25.grid_ref, f32[2,3,144,128]{3,2,1,0:T(8,128)S(1)} %copy-done.1), custom_call_target="tpu_custom_call" | custom-call | tf_op jit(solution)/shard_map/pallas_call | solution.py:546
  60.0 3.7 %all-to-all-start.1 = ((f32[16,24,128]{2,1,0:T(8,128)}), f32[16,24,128]{2,1,0:T(8,128)S(1)}, u32[]{:S(2)}, u32[]{:S(2)}) async-start(f32[16,24,128]{2,1,0:T(8,128)} %get-tuple-element.41), calls=%async_computation.1 | async-start | bytes 393216 | tf_op jit(solution)/shard_map/all_to_all | solution.py:654
  64.4 0.6 reduce_sum.9
  66.3 5.3 %all-to-all-done.1.near_ref = f32[16,24,128]{2,1,0:T(8,128)S(1)} async-done(((f32[16,24,128]{2,1,0:T(8,128)}), f32[16,24,128]{2,1,0:T(8,128)S(1)}, u32[]{:S(2)}, u32[]{:S(2)}) %all-to-all-start.1) | async-done | bytes 196640 | tf_op jit(solution)/shard_map/all_to_all | solution.py:654
  71.6 0.7 copy-done.2
  72.3 20.5 %shard_map.200 = f32[192,128]{1,0:T(8,128)} custom-call(s32[1]{0:T(128)} %bitcast.r_ref, f32[16,24,128]{2,1,0:T(8,128)} %copy-done.2, f32[1,1]{1,0:T(1,128)} %bitcast.11.loss_ref, bf16[384,1024]{1,0:T(8,128)(2,1)} %get-tuple-element.45.wf_a, bf16[384,896]{1,0:T(8,128)(2,1)} %get-tuple-element.46.wf_b, bf16[2,1152,256]{2,1,0:T(8,128)(2,1)} %get-tuple-element.47.wt_ref, ...), custom_call_target="tpu_custom_call" | custom-call | tf_op jit(solution)/shard_map/pallas_call | solution.py:660
  92.8 1.5 %collective-permute-done.3 = f32[192,128]{1,0:T(8,128)S(1)} collective-permute-done((f32[192,128]{1,0:T(8,128)}, f32[192,128]{1,0:T(8,128)S(1)}, u32[]{:S(2)}, u32[]{:S(2)}) %collective-permute-start.3) | collective-permute-done | bytes 98336 | tf_op jit(solution)/shard_map/ppermute | solution.py:403
  94.3 0.9 add.27
  95.2 0.8 collective-permute-start.6
  96.1 2.0 %collective-permute-start.5 = (f32[192,128]{1,0:T(8,128)S(1)}, f32[192,128]{1,0:T(8,128)S(1)}, u32[]{:S(2)}, u32[]{:S(2)}) collective-permute-start(f32[192,128]{1,0:T(8,128)S(1)} %add.27), channel_id=1, source_target_pairs={{0,4},{2,6},{4,0},{6,2},{8,12},{10,14},{12,8},{14,10},{16,20},{18,... | collective-permute-start | bytes 294920 | tf_op jit(solution)/shard_map/ppermute | solution.py:399
  98.1 0.7 collective-permute-start.4
  98.8 3.1 %collective-permute-done.6 = f32[192,128]{1,0:T(8,128)S(1)} collective-permute-done((f32[192,128]{1,0:T(8,128)S(1)}, f32[192,128]{1,0:T(8,128)S(1)}, u32[]{:S(2)}, u32[]{:S(2)}) %collective-permute-start.6) | collective-permute-done | bytes 98336 | tf_op jit(solution)/shard_map/ppermute | solution.py:399
  101.9 1.2 collective-permute-done.5
  103.1 0.6 collective-permute-start.7
  103.7 4.1 %collective-permute-done.7 = f32[192,128]{1,0:T(8,128)S(1)} collective-permute-done((f32[192,128]{1,0:T(8,128)S(1)}, f32[192,128]{1,0:T(8,128)S(1)}, u32[]{:S(2)}, u32[]{:S(2)}) %collective-permute-start.7) | collective-permute-done | bytes 98336 | tf_op jit(solution)/shard_map/ppermute | solution.py:403
  107.8 0.9 collective-permute-start.8
  108.6 5.7 %collective-permute-done.8 = f32[192,128]{1,0:T(8,128)S(1)} collective-permute-done((f32[192,128]{1,0:T(8,128)S(1)}, f32[192,128]{1,0:T(8,128)S(1)}, u32[]{:S(2)}, u32[]{:S(2)}) %collective-permute-start.8) | collective-permute-done | bytes 98336 | tf_op jit(solution)/shard_map/ppermute | solution.py:403
  114.5 0.6 slice.33
  115.1 0.6 slice.39
  115.6 0.6 fusion
  116.3 0.6 copy.39
  116.9 0.6 copy.40
  117.7 0.7 copy.34
  (28 shorter events, 0.6 us)
Async XLA Ops:
  0.6 15.5 %collective-permute-start = (f32[4,12,512]{2,0,1:T(4,128)}, f32[4,12,512]{2,0,1:T(4,128)S(1)}, u32[]{:S(2)}, u32[]{:S(2)}) collective-permute-start(f32[4,12,512]{2,0,1:T(4,128)} %param.14), channel_id=1, source_target_pairs={{0,2},{2,4},{4,6},{6,8},{8,10},{10,12},{12,14},{14,16},{16,18},{18... | collective-permute-start | bytes 294920 | tf_op jit(solution)/shard_map/ppermute | solution.py:575
  5.5 10.7 %collective-permute-start.1 = (f32[4,12,512]{2,0,1:T(4,128)}, f32[4,12,512]{2,0,1:T(4,128)S(1)}, u32[]{:S(2)}, u32[]{:S(2)}) collective-permute-start(f32[4,12,512]{2,0,1:T(4,128)} %param.14), channel_id=1, source_target_pairs={{2,0},{4,2},{6,4},{8,6},{10,8},{12,10},{14,12},{16,14},{18,16},{20... | collective-permute-start | bytes 294920 | tf_op jit(solution)/shard_map/ppermute | solution.py:576
  16.1 33.4 %copy-start.3 = (f32[192,144]{1,0:T(8,128)S(1)}, f32[192,144]{1,0:T(8,128)}, u32[]{:S(2)}) copy-start(f32[192,144]{1,0:T(8,128)} %get-tuple-element.40) | copy-start | bytes 331780
  16.1 41.2 %copy-start = (f32[4,192,192]{2,1,0:T(8,128)S(1)}, f32[4,192,192]{2,1,0:T(8,128)}, u32[]{:S(2)}) copy-start(f32[4,192,192]{2,1,0:T(8,128)} %constant.32.clone.cs_ref) | copy-start | bytes 1769476
  16.1 41.2 %copy-start.1 = (f32[2,3,144,128]{3,2,1,0:T(8,128)S(1)}, f32[2,3,144,128]{3,2,1,0:T(8,128)}, u32[]{:S(2)}) copy-start(f32[2,3,144,128]{3,2,1,0:T(8,128)} %constant.33.clone.sel_ref) | copy-start | bytes 1327108
  16.1 0.6 copy-start.4
  16.2 0.7 copy-start.5
  41.5 15.8 %all-to-all-start = ((f32[16,12,128]{2,1,0:T(8,128)}), f32[16,12,128]{2,1,0:T(8,128)S(1)}, u32[]{:S(2)}, u32[]{:S(2)}) async-start(f32[16,12,128]{2,1,0:T(8,128)} %get-tuple-element.39), calls=%async_computation | async-start | bytes 262144 | tf_op jit(solution)/shard_map/all_to_all | solution.py:650
  49.5 14.8 %copy-start.6 = (f32[1,128]{1,0:T(1,128)S(1)}, f32[1,128]{1,0:T(1,128)}, u32[]{:S(2)}) copy-start(f32[1,128]{1,0:T(1,128)} %get-tuple-element.44) | copy-start | bytes 1540
  49.5 1.5 %collective-permute-start.2 = (f32[192,144]{1,0:T(8,128)S(1)}, f32[192,144]{1,0:T(8,128)S(1)}, u32[]{:S(2)}, u32[]{:S(2)}) collective-permute-start(f32[192,144]{1,0:T(8,128)S(1)} %copy-done.3), channel_id=1, source_target_pairs={{0,1},{1,0},{2,3},{3,2},{4,5},{5,4},{6,7},{7,6},{8,9},{9,8},{10,11... | collective-permute-start | bytes 331784 | tf_op jit(solution)/shard_map/ppermute | solution.py:403
  60.0 11.6 %all-to-all-start.1 = ((f32[16,24,128]{2,1,0:T(8,128)}), f32[16,24,128]{2,1,0:T(8,128)S(1)}, u32[]{:S(2)}, u32[]{:S(2)}) async-start(f32[16,24,128]{2,1,0:T(8,128)} %get-tuple-element.41), calls=%async_computation.1 | async-start | bytes 393216 | tf_op jit(solution)/shard_map/all_to_all | solution.py:654
  71.6 0.7 copy-start.2
  92.7 1.6 %collective-permute-start.3 = (f32[192,128]{1,0:T(8,128)}, f32[192,128]{1,0:T(8,128)S(1)}, u32[]{:S(2)}, u32[]{:S(2)}) collective-permute-start(f32[192,128]{1,0:T(8,128)} %shard_map.200), channel_id=1, source_target_pairs={{0,1},{1,0},{2,3},{3,2},{4,5},{5,4},{6,7},{7,6},{8,9},{9,8},{10,11... | collective-permute-start | bytes 294920 | tf_op jit(solution)/shard_map/ppermute | solution.py:403
  95.2 6.6 %collective-permute-start.6 = (f32[192,128]{1,0:T(8,128)S(1)}, f32[192,128]{1,0:T(8,128)S(1)}, u32[]{:S(2)}, u32[]{:S(2)}) collective-permute-start(f32[192,128]{1,0:T(8,128)S(1)} %add.27), channel_id=1, source_target_pairs={{0,6},{2,4},{4,2},{6,0},{8,14},{10,12},{12,10},{14,8},{16,22},{18,... | collective-permute-start | bytes 294920 | tf_op jit(solution)/shard_map/ppermute | solution.py:399
  96.1 7.0 %collective-permute-start.5 = (f32[192,128]{1,0:T(8,128)S(1)}, f32[192,128]{1,0:T(8,128)S(1)}, u32[]{:S(2)}, u32[]{:S(2)}) collective-permute-start(f32[192,128]{1,0:T(8,128)S(1)} %add.27), channel_id=1, source_target_pairs={{0,4},{2,6},{4,0},{6,2},{8,12},{10,14},{12,8},{14,10},{16,20},{18,... | collective-permute-start | bytes 294920 | tf_op jit(solution)/shard_map/ppermute | solution.py:399
  98.1 4.9 %collective-permute-start.4 = (f32[192,128]{1,0:T(8,128)S(1)}, f32[192,128]{1,0:T(8,128)S(1)}, u32[]{:S(2)}, u32[]{:S(2)}) collective-permute-start(f32[192,128]{1,0:T(8,128)S(1)} %add.27), channel_id=1, source_target_pairs={{0,2},{2,0},{4,6},{6,4},{8,10},{10,8},{12,14},{14,12},{16,18},{18,... | collective-permute-start | bytes 294920 | tf_op jit(solution)/shard_map/ppermute | solution.py:399
  103.1 4.7 %collective-permute-start.7 = (f32[192,128]{1,0:T(8,128)S(1)}, f32[192,128]{1,0:T(8,128)S(1)}, u32[]{:S(2)}, u32[]{:S(2)}) collective-permute-start(f32[192,128]{1,0:T(8,128)S(1)} %add_add_fusion), channel_id=1, source_target_pairs={{0,8},{2,10},{4,12},{6,14},{8,0},{10,2},{12,4},{14,6},{16,24},{18,... | collective-permute-start | bytes 294920 | tf_op jit(solution)/shard_map/ppermute | solution.py:403
  107.8 6.6 %collective-permute-start.8 = (f32[192,128]{1,0:T(8,128)S(1)}, f32[192,128]{1,0:T(8,128)S(1)}, u32[]{:S(2)}, u32[]{:S(2)}) collective-permute-start(f32[192,128]{1,0:T(8,128)S(1)} %add.31), channel_id=1, source_target_pairs={{0,16},{2,18},{4,20},{6,22},{8,24},{10,26},{12,28},{14,30},{16,0},... | collective-permute-start | bytes 294920 | tf_op jit(solution)/shard_map/ppermute | solution.py:403

commit v4 on v3

--- a/solution.py
+++ b/solution.py
@@ -405,7 +405,7 @@
     return value
 
 
-def grid_kernel(n_freq, pad_freq, height, img_width, r_ref, u_ref, v_ref, obs_ref, w_ref, out_ref, const_ref,
+def grid_kernel(n_freq, pad_freq, height, img_width, r_ref, g_ref, u_ref, v_ref, obs_ref, w_ref, out_ref, const_ref,
                 u_s, c_s, sign_s):
     share = u_s.shape[0]
     half = img_width // 2
@@ -475,25 +475,25 @@
     pad_freq = slot_count(n_freq)
     rows = vis_u.shape[0] // LANE
     share = rows // n_grp
-    rows_spec = pl.BlockSpec((share, LANE), lambda i, r: (r[1], 0))
-    where = jnp.stack([lax.axis_index("rows"), lax.axis_index("grp")]).astype(jnp.int32)
+    rows_spec = pl.BlockSpec((share, LANE), lambda i, r, g: (g[0], 0))
+    where = [lax.axis_index(axis)[None].astype(jnp.int32) for axis in ("rows", "grp")]
     return pl.pallas_call(
         functools.partial(grid_kernel, n_freq, pad_freq, height, img_width),
         out_shape=(jax.ShapeDtypeStruct((height, 6 * pad_freq), F32),
                    jax.ShapeDtypeStruct((1, 1), F32)),
         grid_spec=pltpu.PrefetchScalarGridSpec(
-            num_scalar_prefetch=1,
+            num_scalar_prefetch=2,
             grid=(1,),
-            in_specs=[rows_spec, rows_spec, pl.BlockSpec((2, share * LANE), lambda i, r: (0, r[1])), rows_spec],
-            out_specs=(pl.BlockSpec((height, 6 * pad_freq), lambda i, r: (0, 0)),
-                       pl.BlockSpec((1, 1), lambda i, r: (0, 0))),
+            in_specs=[rows_spec, rows_spec, pl.BlockSpec((2, share * LANE), lambda i, r, g: (0, g[0])), rows_spec],
+            out_specs=(pl.BlockSpec((height, 6 * pad_freq), lambda i, r, g: (0, 0)),
+                       pl.BlockSpec((1, 1), lambda i, r, g: (0, 0))),
             scratch_shapes=[pltpu.VMEM((share, LANE), jnp.int32), pltpu.VMEM((share, LANE), jnp.int32),
                             pltpu.VMEM((share, LANE), F32)],
         ),
         compiler_params=pltpu.CompilerParams(vmem_limit_bytes=60 * 2**20),
         cost_estimate=pl.CostEstimate(flops=2 * height * 256 * share * LANE * 4,
                                       bytes_accessed=24 * share * LANE, transcendentals=0),
-    )(where, vis_u.reshape(rows, LANE), vis_v.reshape(rows, LANE), observed, vis_weight.reshape(rows, LANE))
+    )(*where, vis_u.reshape(rows, LANE), vis_v.reshape(rows, LANE), observed, vis_weight.reshape(rows, LANE))
 
 
 def column_basis(img_width):

time: 119 us -> 118 us (level)
  no operation moved by 1% of the time
where the time goes in v4:
time: 118 us; the launch traced here: 117 us
  Pallas kernels  55.9 us (47%)
  waiting for transfers between devices  28.5 us (24%)
  starting transfers between devices  23.1 us (20%)
  local copies, waits for them, and re-layouts  5.34 us (5%)
  between operations  2.79 us (2%)
  other arithmetic  1.59 us (1%)
    pallas_call x1, Pallas kernels, body(): pl.pallas_call(functools.partial(forward_kernel, height, row_count, chann...  24.7 us
    pallas_call x1, Pallas kernels, body(): pl.pallas_call(functools.partial(backward_kernel, height, row_count, chan...  20.5 us
    ppermute x4, waiting for transfers between devices, butterfly(): lax.ppermute(value, axis, [(i, i ^ hop) for i in range(count)])  12.7 us
    pallas_call x1, Pallas kernels, gridded(): pl.pallas_call(functools.partial(grid_kernel, n_freq, pad_freq, height, i...  8.06 us
    all_to_all x1, starting transfers between devices, body(): columns = lax.all_to_all(columns, 'rows', 0, 0, tiled=True)  8.03 us
    all_to_all x1, waiting for transfers between devices, body(): columns = lax.all_to_all(columns, 'rows', 0, 0, tiled=True)  6.23 us
    all_to_all x1, waiting for transfers between devices, body(): near = lax.all_to_all(near, 'rows', 0, 0, tiled=True)  5.3 us
    ppermute x1, starting transfers between devices, body(): low = lax.ppermute(latent, 'rows', forward)  4.85 us
  transfers between devices with their start and end apart: 11, of which 8 were waited for; matrix products, arithmetic and copies ran while one was open for 1% of the time, Pallas kernels for 7%

profile of v4, /device:TPU:0, one launch (start us, length us, event | category | flops | bytes accessed | tf_op | source)
XLA Modules:
  0.0 117.2 jit_solution(7535682511570606423)
XLA Ops:
  0.6 4.8 %collective-permute-start = (f32[4,12,512]{2,0,1:T(4,128)}, f32[4,12,512]{2,0,1:T(4,128)S(1)}, u32[]{:S(2)}, u32[]{:S(2)}) collective-permute-start(f32[4,12,512]{2,0,1:T(4,128)} %param.14), channel_id=1, source_target_pairs={{0,2},{2,4},{4,6},{6,8},{8,10},{10,12},{12,14},{14,16},{16,18},{18... | collective-permute-start | bytes 294920 | tf_op jit(solution)/shard_map/ppermute | solution.py:575
  5.5 1.3 %collective-permute-start.1 = (f32[4,12,512]{2,0,1:T(4,128)}, f32[4,12,512]{2,0,1:T(4,128)S(1)}, u32[]{:S(2)}, u32[]{:S(2)}) collective-permute-start(f32[4,12,512]{2,0,1:T(4,128)} %param.14), channel_id=1, source_target_pairs={{2,0},{4,2},{6,4},{8,6},{10,8},{12,10},{14,12},{16,14},{18,16},{20... | collective-permute-start | bytes 294920 | tf_op jit(solution)/shard_map/ppermute | solution.py:576
  6.8 8.1 %shard_map.197 = (f32[192,144]{1,0:T(8,128)}, f32[1,1]{1,0:T(1,128)}) custom-call(s32[1]{0:T(128)} %bitcast.r_ref, s32[1]{0:T(128)} %bitcast.1.g_ref, s32[512,128]{1,0:T(8,128)} %bitcast.45, s32[512,128]{1,0:T(8,128)} %bitcast.46, f32[2,65536]{1,0:T(2,128)} %obs_ref.1, f32[512,128]{1,0:T(8,128)} %bitcast.47), custom_call_target="tpu_custom_call" | custom-call | flops 12884901888 | bytes 786432 | tf_op jit(solution)/shard_map/pallas_call | solution.py:480
  14.9 0.6 copy-done.4
  15.6 24.7 %shard_map.198 = (f32[12,4,512]{2,1,0:T(4,128)}, f32[16,12,128]{2,1,0:T(8,128)}, f32[1,128]{1,0:T(1,128)}, bf16[384,1024]{1,0:T(8,128)(2,1)}, bf16[384,896]{1,0:...) custom-call(s32[1]{0:T(128)} %bitcast.r_ref, ...), custom_call_target="tpu_custom_call" | custom-call | tf_op jit(solution)/shard_map/pallas_call | solution.py:616
  40.2 8.0 %all-to-all-start = ((f32[16,12,128]{2,1,0:T(8,128)}), f32[16,12,128]{2,1,0:T(8,128)S(1)}, u32[]{:S(2)}, u32[]{:S(2)}) async-start(f32[16,12,128]{2,1,0:T(8,128)} %get-tuple-element.39), calls=%async_computation | async-start | bytes 262144 | tf_op jit(solution)/shard_map/all_to_all | solution.py:650
  48.4 1.4 %collective-permute-done.2 = f32[192,144]{1,0:T(8,128)S(1)} collective-permute-done((f32[192,144]{1,0:T(8,128)S(1)}, f32[192,144]{1,0:T(8,128)S(1)}, u32[]{:S(2)}, u32[]{:S(2)}) %collective-permute-start.2) | collective-permute-done | bytes 110624 | tf_op jit(solution)/shard_map/ppermute | solution.py:403
  49.8 6.2 %all-to-all-done = f32[16,12,128]{2,1,0:T(8,128)S(1)} async-done(((f32[16,12,128]{2,1,0:T(8,128)}), f32[16,12,128]{2,1,0:T(8,128)S(1)}, u32[]{:S(2)}, u32[]{:S(2)}) %all-to-all-start) | async-done | bytes 98336 | tf_op jit(solution)/shard_map/all_to_all | solution.py:650
  56.1 2.7 %shard_map.199 = (f32[16,24,128]{2,1,0:T(8,128)}, f32[1,1]{1,0:T(1,128)}) custom-call(s32[1]{0:T(128)} %bitcast.r_ref, f32[192,128]{1,0:T(8,128)S(1)} %reshape.58.z_ref, f32[4,192,192]{2,1,0:T(8,128)S(1)} %copy-done, f32[192,144]{1,0:T(8,128)S(1)} %add.25.grid_ref, f32[2,3,144,128]{3,2,1,0:T(8,128)S(1)} %copy-done.1), custom_call_target="tpu_custom_call" | custom-call | tf_op jit(solution)/shard_map/pallas_call | solution.py:546
  58.7 3.7 %all-to-all-start.1 = ((f32[16,24,128]{2,1,0:T(8,128)}), f32[16,24,128]{2,1,0:T(8,128)S(1)}, u32[]{:S(2)}, u32[]{:S(2)}) async-start(f32[16,24,128]{2,1,0:T(8,128)} %get-tuple-element.41), calls=%async_computation.1 | async-start | bytes 393216 | tf_op jit(solution)/shard_map/all_to_all | solution.py:654
  63.1 0.6 reduce_sum.9
  65.0 5.3 %all-to-all-done.1.near_ref = f32[16,24,128]{2,1,0:T(8,128)S(1)} async-done(((f32[16,24,128]{2,1,0:T(8,128)}), f32[16,24,128]{2,1,0:T(8,128)S(1)}, u32[]{:S(2)}, u32[]{:S(2)}) %all-to-all-start.1) | async-done | bytes 196640 | tf_op jit(solution)/shard_map/all_to_all | solution.py:654
  70.3 0.7 copy-done.2
  71.0 20.5 %shard_map.200 = f32[192,128]{1,0:T(8,128)} custom-call(s32[1]{0:T(128)} %bitcast.r_ref, f32[16,24,128]{2,1,0:T(8,128)} %copy-done.2, f32[1,1]{1,0:T(1,128)} %bitcast.11.loss_ref, bf16[384,1024]{1,0:T(8,128)(2,1)} %get-tuple-element.45.wf_a, bf16[384,896]{1,0:T(8,128)(2,1)} %get-tuple-element.46.wf_b, bf16[2,1152,256]{2,1,0:T(8,128)(2,1)} %get-tuple-element.47.wt_ref, ...), custom_call_target="tpu_custom_call" | custom-call | tf_op jit(solution)/shard_map/pallas_call | solution.py:660
  91.6 1.5 %collective-permute-done.3 = f32[192,128]{1,0:T(8,128)S(1)} collective-permute-done((f32[192,128]{1,0:T(8,128)}, f32[192,128]{1,0:T(8,128)S(1)}, u32[]{:S(2)}, u32[]{:S(2)}) %collective-permute-start.3) | collective-permute-done | bytes 98336 | tf_op jit(solution)/shard_map/ppermute | solution.py:403
  93.1 0.9 add.27
  94.0 0.8 collective-permute-start.6
  94.8 2.0 %collective-permute-start.5 = (f32[192,128]{1,0:T(8,128)S(1)}, f32[192,128]{1,0:T(8,128)S(1)}, u32[]{:S(2)}, u32[]{:S(2)}) collective-permute-start(f32[192,128]{1,0:T(8,128)S(1)} %add.27), channel_id=1, source_target_pairs={{0,4},{2,6},{4,0},{6,2},{8,12},{10,14},{12,8},{14,10},{16,20},{18,... | collective-permute-start | bytes 294920 | tf_op jit(solution)/shard_map/ppermute | solution.py:399
  96.8 0.7 collective-permute-start.4
  97.5 3.1 %collective-permute-done.6 = f32[192,128]{1,0:T(8,128)S(1)} collective-permute-done((f32[192,128]{1,0:T(8,128)S(1)}, f32[192,128]{1,0:T(8,128)S(1)}, u32[]{:S(2)}, u32[]{:S(2)}) %collective-permute-start.6) | collective-permute-done | bytes 98336 | tf_op jit(solution)/shard_map/ppermute | solution.py:399
  100.6 1.2 collective-permute-done.5
  101.8 0.6 collective-permute-start.7
  102.4 4.1 %collective-permute-done.7 = f32[192,128]{1,0:T(8,128)S(1)} collective-permute-done((f32[192,128]{1,0:T(8,128)S(1)}, f32[192,128]{1,0:T(8,128)S(1)}, u32[]{:S(2)}, u32[]{:S(2)}) %collective-permute-start.7) | collective-permute-done | bytes 98336 | tf_op jit(solution)/shard_map/ppermute | solution.py:403
  106.5 0.9 collective-permute-start.8
  107.4 5.7 %collective-permute-done.8 = f32[192,128]{1,0:T(8,128)S(1)} collective-permute-done((f32[192,128]{1,0:T(8,128)S(1)}, f32[192,128]{1,0:T(8,128)S(1)}, u32[]{:S(2)}, u32[]{:S(2)}) %collective-permute-start.8) | collective-permute-done | bytes 98336 | tf_op jit(solution)/shard_map/ppermute | solution.py:403
  113.2 0.6 slice.33
  113.8 0.6 slice.39
  114.4 0.6 fusion
  115.0 0.6 copy.39
  115.6 0.6 copy.40
  116.2 0.2 reshape.62
  116.4 0.7 copy.34
  (27 shorter events, 0.4 us)
Async XLA Ops:
  0.6 14.2 %collective-permute-start = (f32[4,12,512]{2,0,1:T(4,128)}, f32[4,12,512]{2,0,1:T(4,128)S(1)}, u32[]{:S(2)}, u32[]{:S(2)}) collective-permute-start(f32[4,12,512]{2,0,1:T(4,128)} %param.14), channel_id=1, source_target_pairs={{0,2},{2,4},{4,6},{6,8},{8,10},{10,12},{12,14},{14,16},{16,18},{18... | collective-permute-start | bytes 294920 | tf_op jit(solution)/shard_map/ppermute | solution.py:575
  5.5 9.4 %collective-permute-start.1 = (f32[4,12,512]{2,0,1:T(4,128)}, f32[4,12,512]{2,0,1:T(4,128)S(1)}, u32[]{:S(2)}, u32[]{:S(2)}) collective-permute-start(f32[4,12,512]{2,0,1:T(4,128)} %param.14), channel_id=1, source_target_pairs={{2,0},{4,2},{6,4},{8,6},{10,8},{12,10},{14,12},{16,14},{18,16},{20... | collective-permute-start | bytes 294920 | tf_op jit(solution)/shard_map/ppermute | solution.py:576
  14.9 33.4 %copy-start.3 = (f32[192,144]{1,0:T(8,128)S(1)}, f32[192,144]{1,0:T(8,128)}, u32[]{:S(2)}) copy-start(f32[192,144]{1,0:T(8,128)} %get-tuple-element.40) | copy-start | bytes 331780
  14.9 41.2 %copy-start = (f32[4,192,192]{2,1,0:T(8,128)S(1)}, f32[4,192,192]{2,1,0:T(8,128)}, u32[]{:S(2)}) copy-start(f32[4,192,192]{2,1,0:T(8,128)} %constant.32.clone.cs_ref) | copy-start | bytes 1769476
  14.9 41.2 %copy-start.1 = (f32[2,3,144,128]{3,2,1,0:T(8,128)S(1)}, f32[2,3,144,128]{3,2,1,0:T(8,128)}, u32[]{:S(2)}) copy-start(f32[2,3,144,128]{3,2,1,0:T(8,128)} %constant.33.clone.sel_ref) | copy-start | bytes 1327108
  14.9 0.6 copy-start.4
  14.9 0.7 copy-start.5
  40.2 15.8 %all-to-all-start = ((f32[16,12,128]{2,1,0:T(8,128)}), f32[16,12,128]{2,1,0:T(8,128)S(1)}, u32[]{:S(2)}, u32[]{:S(2)}) async-start(f32[16,12,128]{2,1,0:T(8,128)} %get-tuple-element.39), calls=%async_computation | async-start | bytes 262144 | tf_op jit(solution)/shard_map/all_to_all | solution.py:650
  48.3 14.8 %copy-start.6 = (f32[1,128]{1,0:T(1,128)S(1)}, f32[1,128]{1,0:T(1,128)}, u32[]{:S(2)}) copy-start(f32[1,128]{1,0:T(1,128)} %get-tuple-element.44) | copy-start | bytes 1540
  48.3 1.5 %collective-permute-start.2 = (f32[192,144]{1,0:T(8,128)S(1)}, f32[192,144]{1,0:T(8,128)S(1)}, u32[]{:S(2)}, u32[]{:S(2)}) collective-permute-start(f32[192,144]{1,0:T(8,128)S(1)} %copy-done.3), channel_id=1, source_target_pairs={{0,1},{1,0},{2,3},{3,2},{4,5},{5,4},{6,7},{7,6},{8,9},{9,8},{10,11... | collective-permute-start | bytes 331784 | tf_op jit(solution)/shard_map/ppermute | solution.py:403
  58.7 11.6 %all-to-all-start.1 = ((f32[16,24,128]{2,1,0:T(8,128)}), f32[16,24,128]{2,1,0:T(8,128)S(1)}, u32[]{:S(2)}, u32[]{:S(2)}) async-start(f32[16,24,128]{2,1,0:T(8,128)} %get-tuple-element.41), calls=%async_computation.1 | async-start | bytes 393216 | tf_op jit(solution)/shard_map/all_to_all | solution.py:654
  70.3 0.7 copy-start.2
  91.5 1.6 %collective-permute-start.3 = (f32[192,128]{1,0:T(8,128)}, f32[192,128]{1,0:T(8,128)S(1)}, u32[]{:S(2)}, u32[]{:S(2)}) collective-permute-start(f32[192,128]{1,0:T(8,128)} %shard_map.200), channel_id=1, source_target_pairs={{0,1},{1,0},{2,3},{3,2},{4,5},{5,4},{6,7},{7,6},{8,9},{9,8},{10,11... | collective-permute-start | bytes 294920 | tf_op jit(solution)/shard_map/ppermute | solution.py:403
  94.0 6.6 %collective-permute-start.6 = (f32[192,128]{1,0:T(8,128)S(1)}, f32[192,128]{1,0:T(8,128)S(1)}, u32[]{:S(2)}, u32[]{:S(2)}) collective-permute-start(f32[192,128]{1,0:T(8,128)S(1)} %add.27), channel_id=1, source_target_pairs={{0,6},{2,4},{4,2},{6,0},{8,14},{10,12},{12,10},{14,8},{16,22},{18,... | collective-permute-start | bytes 294920 | tf_op jit(solution)/shard_map/ppermute | solution.py:399
  94.8 7.0 %collective-permute-start.5 = (f32[192,128]{1,0:T(8,128)S(1)}, f32[192,128]{1,0:T(8,128)S(1)}, u32[]{:S(2)}, u32[]{:S(2)}) collective-permute-start(f32[192,128]{1,0:T(8,128)S(1)} %add.27), channel_id=1, source_target_pairs={{0,4},{2,6},{4,0},{6,2},{8,12},{10,14},{12,8},{14,10},{16,20},{18,... | collective-permute-start | bytes 294920 | tf_op jit(solution)/shard_map/ppermute | solution.py:399
  96.8 4.9 %collective-permute-start.4 = (f32[192,128]{1,0:T(8,128)S(1)}, f32[192,128]{1,0:T(8,128)S(1)}, u32[]{:S(2)}, u32[]{:S(2)}) collective-permute-start(f32[192,128]{1,0:T(8,128)S(1)} %add.27), channel_id=1, source_target_pairs={{0,2},{2,0},{4,6},{6,4},{8,10},{10,8},{12,14},{14,12},{16,18},{18,... | collective-permute-start | bytes 294920 | tf_op jit(solution)/shard_map/ppermute | solution.py:399
  101.8 4.7 %collective-permute-start.7 = (f32[192,128]{1,0:T(8,128)S(1)}, f32[192,128]{1,0:T(8,128)S(1)}, u32[]{:S(2)}, u32[]{:S(2)}) collective-permute-start(f32[192,128]{1,0:T(8,128)S(1)} %add_add_fusion), channel_id=1, source_target_pairs={{0,8},{2,10},{4,12},{6,14},{8,0},{10,2},{12,4},{14,6},{16,24},{18,... | collective-permute-start | bytes 294920 | tf_op jit(solution)/shard_map/ppermute | solution.py:403
  106.5 6.6 %collective-permute-start.8 = (f32[192,128]{1,0:T(8,128)S(1)}, f32[192,128]{1,0:T(8,128)S(1)}, u32[]{:S(2)}, u32[]{:S(2)}) collective-permute-start(f32[192,128]{1,0:T(8,128)S(1)} %add.31), channel_id=1, source_target_pairs={{0,16},{2,18},{4,20},{6,22},{8,24},{10,26},{12,28},{14,30},{16,0},... | collective-permute-start | bytes 294920 | tf_op jit(solution)/shard_map/ppermute | solution.py:403
